TPU v7x, 128 devices: a whole 4x4x4 slice. The times are simulated.
128 devices in a mesh: batch: 8 (over x, z_lo), grid: 16 (over y, z_hi, core).
Axes of the slice: x: 4, y: 4, z: 4 (z_hi: 2, z_lo: 2; z = z_hi * 2 + z_lo), core: 2. Of those that a mesh axis runs over, the one named last changes fastest.
Arguments:
- samples: bfloat16 [8192, 1024], P('batch'), may hold values from -6 to 6
- point_index: int32 [2, 65536], P(None, 'grid'), may hold values from 0 to 8191
- targets: bfloat16 [8192, 65536], P('batch', 'grid'), may hold values from -6 to 6
- w_in: bfloat16 [1024, 256], replicated, may hold values from -0.1875 to 0.1875
- w_mid: bfloat16 [256, 256], replicated, may hold values from -0.375 to 0.375
- w_out: bfloat16 [256, 256], replicated, may hold values from -0.375 to 0.375
- v_in: bfloat16 [256, 256], replicated, may hold values from -0.375 to 0.375
- v_mid: bfloat16 [256, 256], replicated, may hold values from -0.375 to 0.375
- v_out: bfloat16 [256, 256], replicated, may hold values from -0.375 to 0.375
Outputs:
- grad_w_in: float32 [1024, 256], replicated
- grad_w_mid: float32 [256, 256], replicated
- grad_w_out: float32 [256, 256], replicated
- grad_v_in: float32 [256, 256], replicated
- grad_v_mid: float32 [256, 256], replicated
- grad_v_out: float32 [256, 256], replicated
- loss: float32 [], replicated
All inputs are finite; a program needn't handle non-finite values.
Results may differ from a plain program's by a relative error of at most 0.004.
Values may be sent and summed in bfloat16 or wider, within the bound.
A program may use at most 128 MiB of HBM per device.

v0:
```python
import math

import jax
import jax.numpy as jnp
from jax import lax
from jax.sharding import PartitionSpec as P

GRID_SIDE = 8192


def fourier_features(point_index, feat_count):
    quarter = feat_count // 4
    frequency = math.pi * (jnp.arange(quarter, dtype=jnp.float32) + 1.0)
    first_coord = (point_index[0].astype(jnp.float32) + 0.5) / GRID_SIDE
    second_coord = (point_index[1].astype(jnp.float32) + 0.5) / GRID_SIDE
    phase_one = first_coord[:, None] * frequency[None, :]
    phase_two = second_coord[:, None] * frequency[None, :]
    joined = jnp.concatenate(
        [jnp.sin(phase_one), jnp.cos(phase_one), jnp.sin(phase_two), jnp.cos(phase_two)], axis=1
    )
    return joined.astype(jnp.bfloat16)


def contract_rows(left_side, right_side):
    return lax.dot_general(
        left_side, right_side, (((0,), (0,)), ((), ())), preferred_element_type=jnp.float32
    )


def contract_cols(left_side, right_side):
    return lax.dot_general(
        left_side, right_side, (((1,), (1,)), ((), ())), preferred_element_type=jnp.float32
    )


def network_forward(inputs, w_first, w_middle, w_last):
    hidden_one = jnp.tanh(jnp.dot(inputs, w_first, preferred_element_type=jnp.float32)).astype(
        jnp.bfloat16
    )
    hidden_two = jnp.tanh(jnp.dot(hidden_one, w_middle, preferred_element_type=jnp.float32)).astype(
        jnp.bfloat16
    )
    output = jnp.dot(hidden_two, w_last, preferred_element_type=jnp.float32).astype(jnp.bfloat16)
    return (hidden_one, hidden_two, output)


def network_backward(inputs, hidden_one, hidden_two, w_middle, w_last, out_grad):
    grad_last = contract_rows(hidden_two, out_grad)
    slope_two = 1.0 - jnp.square(hidden_two.astype(jnp.float32))
    back_two = (contract_cols(out_grad, w_last) * slope_two).astype(jnp.bfloat16)
    grad_middle = contract_rows(hidden_one, back_two)
    slope_one = 1.0 - jnp.square(hidden_one.astype(jnp.float32))
    back_one = (contract_cols(back_two, w_middle) * slope_one).astype(jnp.bfloat16)
    grad_first = contract_rows(inputs, back_one)
    return (grad_first, grad_middle, grad_last)


def on_device(samples, point_index, targets, w_in, w_mid, w_out, v_in, v_mid, v_out):
    grid_count = lax.axis_size("grid")
    batch_count = lax.axis_size("batch")
    samp_local, pts_local = targets.shape
    total_cells = samp_local * batch_count * pts_local * grid_count
    coef_width = w_out.shape[1]
    width_scale = coef_width ** (-0.5)
    grad_factor = 64.0 / math.sqrt(total_cells) * width_scale
    own_samples = samp_local // grid_count
    samp_start = lax.axis_index("grid") * own_samples
    own_points = pts_local // batch_count
    point_start = lax.axis_index("batch") * own_points
    input_all = fourier_features(point_index, v_in.shape[0])
    one_all, two_all, trunk_basis = network_forward(input_all, v_in, v_mid, v_out)
    trunk_input = lax.dynamic_slice_in_dim(input_all, point_start, own_points, 0)
    trunk_one = lax.dynamic_slice_in_dim(one_all, point_start, own_points, 0)
    trunk_two = lax.dynamic_slice_in_dim(two_all, point_start, own_points, 0)
    samples_own = lax.dynamic_slice_in_dim(samples, samp_start, own_samples, 0)
    branch_one, branch_two, coeff_own = network_forward(samples_own, w_in, w_mid, w_out)
    shard_rows = lax.all_gather(coeff_own, "grid", axis=0, tiled=True)
    predicted = contract_cols(shard_rows, trunk_basis) * width_scale
    residual = predicted - targets.astype(jnp.float32)
    pred_grad = (residual * grad_factor).astype(jnp.bfloat16)
    coeff_part = jnp.dot(pred_grad, trunk_basis, preferred_element_type=jnp.float32)
    coeff_sum = coeff_part
    basis_sum = contract_rows(pred_grad, shard_rows)
    square_sum = jnp.sum(residual * residual)
    coeff_sum, basis_sum, square_sum = (coeff_sum, basis_sum, square_sum)
    coeff_grad = lax.psum_scatter(coeff_sum, "grid", scatter_dimension=0, tiled=True).astype(
        jnp.bfloat16
    )
    basis_grad = lax.psum_scatter(
        basis_sum.astype(jnp.bfloat16), "batch", scatter_dimension=0, tiled=True
    )
    part_w_in, part_w_mid, part_w_out = network_backward(
        samples_own, branch_one, branch_two, w_mid, w_out, coeff_grad
    )
    part_v_in, part_v_mid, part_v_out = network_backward(
        trunk_input, trunk_one, trunk_two, v_mid, v_out, basis_grad
    )
    summed = lax.psum(
        (part_w_in, part_w_mid, part_w_out, part_v_in, part_v_mid, part_v_out, square_sum),
        ("batch", "grid"),
    )
    loss = summed[6] / (2.0 * total_cells)
    return (summed[0], summed[1], summed[2], summed[3], summed[4], summed[5], loss)


def solution(mesh):
    placed = (P("batch", None), P(None, "grid"), P("batch", "grid"), P(), P(), P(), P(), P(), P())
    return jax.shard_map(
        on_device,
        mesh=mesh,
        in_specs=placed,
        out_specs=(P(), P(), P(), P(), P(), P(), P()),
        check_vma=False,
    )
```

profile of v0, /device:TPU:1, one launch (start us, length us, event | category | flops | bytes accessed | tf_op | source)
XLA Modules:
  0.0 371.1 jit_solution(8636958579270331199)
XLA Ops:
  7.2 1.0 add_multiply_fusion.1
  8.8 1.3 fusion.5
  10.1 1.1 fusion.6
  11.2 1.1 convolution_convert_fusion.2
  12.2 28.3 %all_gather.3 = bf16[1024,256]{1,0:T(8,128)(2,1)S(1)} all-gather(bf16[64,256]{1,0:T(8,128)(2,1)S(1)} %convolution_convert_fusion.2), channel_id=1, replica_groups=mesh['batch'=8,'grid'=16] {'grid'}, dimensions={0}, use_global_device_ids=true | all-gather | bytes 557056 | tf_op jit(solution)/shard_map/all_gather | solution.py:77
  40.5 7.7 %fusion.10 = (bf16[4096,64]{0,1:T(8,128)(2,1)S(1)}, bf16[4096,64]{0,1:T(8,128)(2,1)S(1)}, bf16[4096,64]{0,1:T(8,128)(2,1)S(1)}, bf16[4096,64]{0,1:T(8,128)(2,1)S(1)}) fusion(f32[64]{0:T(128)S(1)} %add_multiply_fusion.2, f32[4096]{0:T(1024)S(1)} %bitcast.28, f32[4096]{0:T(1024)S(1)} %bitcast.29), kind=kLoop, calls=%fused_computation.29 | loop fusion | flops 1572864 | bytes 2130176 | tf_op jit(solution)/shard_map/convert
  48.3 2.1 fusion
  50.5 0.7 fusion.1
  51.8 1.3 copy-done.3
  53.1 0.7 convolution_convert_fusion.1
  53.8 8.6 %multiply_reduce_fusion = (f32[]{:T(128)}, f32[1024,4096]{1,0:T(8,128)S(1)}) fusion(bf16[1024,4096]{1,0:T(8,128)(2,1)} %param.11, bf16[1024,256]{1,0:T(8,128)(2,1)S(1)} %all_gather.3, bf16[4096,256]{1,0:T(8,128)(2,1)S(1)} %convolution_convert_fusion.1), kind=kOutput, calls=%fused_computation | convolution fusion | flops 2168455168 | bytes 27787268 | tf_op jit(solution)/shard_map/dot_general | solution.py:31
  62.4 5.7 %copy-done.1 = f32[1024,4096]{1,0:T(8,128)} copy-done((f32[1024,4096]{1,0:T(8,128)}, f32[1024,4096]{1,0:T(8,128)S(1)}, u32[]{:S(2)}) %copy-start.1) | copy-done | bytes 16777240
  68.1 7.9 %fusion.40 = f32[1024,256]{1,0:T(8,128)} fusion(bf16[4096,256]{1,0:T(8,128)(2,1)} %copy-done.2, bf16[1024,4096]{1,0:T(8,128)(2,1)} %param.11, f32[1024,4096]{1,0:T(8,128)S(1)} %get-tuple-element.22), kind=kOutput, calls=%fused_computation.62 | convolution fusion | flops 2168455168 | bytes 28311552 | tf_op jit(solution)/shard_map/dot_general | solution.py:81
  76.3 13.8 %convolution_convert_fusion = bf16[4096,256]{1,0:T(8,128)(2,1)} fusion(bf16[1024,256]{1,0:T(8,128)(2,1)S(1)} %all_gather.3, bf16[1024,4096]{1,0:T(8,128)(2,1)} %param.11, f32[1024,4096]{1,0:T(8,128)} %copy-done.1), kind=kOutput, calls=%fused_computation.5 | convolution fusion | flops 2169503744 | bytes 27787264 | tf_op jit(solution)/shard_map/dot_general | solution.py:25
  90.2 3.1 pad_maximum_fusion
  93.3 43.7 %reduce-scatter.3.cloned.1.call-done = f32[64,256]{1,0:T(8,128)} async-done(((f32[1024,256]{1,0:T(8,128)}), f32[64,256]{1,0:T(8,128)}) %reduce-scatter.3.cloned.1.call-update) | async-done | bytes 65552 | tf_op jit(solution)/shard_map/reduce_scatter | solution.py:86
  137.0 1.0 fusion.7
  138.1 0.9 fusion.41
  139.0 1.8 fusion.30
  140.7 1.5 fusion.9
  142.2 48.8 %reduce-scatter.5.cloned.1.call-done = bf16[512,256]{1,0:T(8,128)(2,1)} async-done(((bf16[4096,256]{1,0:T(8,128)(2,1)}), bf16[512,256]{1,0:T(8,128)(2,1)}) %reduce-scatter.5.cloned.1.call-update) | async-done | bytes 262160 | tf_op jit(solution)/shard_map/reduce_scatter | solution.py:89
  191.0 1.3 fusion.2
  192.3 1.9 fusion.19
  194.3 2.2 fusion.4
  196.5 2.0 fusion.22
  198.5 66.7 %psum.55 = f32[]{:T(128)} all-reduce(f32[]{:T(128)} %get-tuple-element.21), channel_id=1, replica_groups=mesh['batch'=8,'grid'=16] {'batch','grid'}, use_global_device_ids=true, to_apply=%region_9.0 | all-reduce | flops 1 | bytes 8 | tf_op jit(solution)/shard_map/psum | solution.py:98
  265.9 87.9 %all-reduce.3.cloned.1.call-done = (f32[1024,256]{1,0:T(8,128)}, f32[256,256]{1,0:T(8,128)}, f32[256,256]{1,0:T(8,128)}, f32[256,256]{1,0:T(8,128)}, f32[256,256]{1,0:T(8,128)}, /*index=5*/f32[256,256]{1,0:T(8,128)}) async-done(((f32[1024,256]{1,0:T(8,128)}, f32[256,256]{1,0:T(8,128)}, f32[256,256]{1,0:T(8,128)}, f32[256,256]{1,0:T(8,128)}, f32[256,256]{1,0:T(8,128)}, /*index=5*/f32[256,256]{1,0:T(8,128)}), ...) | async-done | bytes 2359312 | tf_op jit(solution)/shard_map/psum | solution.py:98
  353.8 2.3 copy.22
  356.1 1.7 copy.23
  357.8 1.7 copy.24
  359.4 1.7 copy.25
  361.1 1.7 copy.26
  (48 shorter events, 2.3 us)
Async XLA Ops:
  7.2 1.6 copy-start
  7.2 129.8 %reduce-scatter.3.cloned.1.call-start = ((), (), s32[]{:S(2)}) async-start(), calls=%async_computation.2 | async-start | bytes 1114112 | tf_op jit(solution)/shard_map/reduce_scatter | solution.py:86
  10.1 38.2 %copy-start.11 = (bf16[64,256]{1,0:T(8,128)(2,1)}, bf16[64,256]{1,0:T(8,128)(2,1)S(1)}, u32[]{:S(2)}) copy-start(bf16[64,256]{1,0:T(8,128)(2,1)S(1)} %fusion.5) | copy-start | bytes 98308
  11.2 37.1 %copy-start.14 = (bf16[64,256]{1,0:T(8,128)(2,1)}, bf16[64,256]{1,0:T(8,128)(2,1)S(1)}, u32[]{:S(2)}) copy-start(bf16[64,256]{1,0:T(8,128)(2,1)S(1)} %fusion.6) | copy-start | bytes 98308
  48.2 2.2 copy-start.5
  48.2 2.2 copy-start.7
  48.2 2.2 copy-start.8
  48.2 2.2 copy-start.9
  48.3 2.2 copy-start.19
  50.5 1.3 copy-start.4
  50.5 2.6 copy-start.17
  51.8 1.3 copy-start.3
  53.8 8.6 %copy-start.2 = (bf16[4096,256]{1,0:T(8,128)(2,1)}, bf16[4096,256]{1,0:T(8,128)(2,1)S(1)}, u32[]{:S(2)}) copy-start(bf16[4096,256]{1,0:T(8,128)(2,1)S(1)} %convolution_convert_fusion.1) | copy-start | bytes 6291460
  62.4 5.7 %copy-start.1 = (f32[1024,4096]{1,0:T(8,128)}, f32[1024,4096]{1,0:T(8,128)S(1)}, u32[]{:S(2)}) copy-start(f32[1024,4096]{1,0:T(8,128)S(1)} %get-tuple-element.22) | copy-start | bytes 50331652
  76.0 14.2 %copy-start.6 = (bf16[4096,64]{0,1:T(8,128)(2,1)S(1)}, bf16[4096,64]{0,1:T(8,128)(2,1)}, u32[]{:S(2)}) copy-start(bf16[4096,64]{0,1:T(8,128)(2,1)} %copy-done.5) | copy-start | bytes 1572868
  76.0 115.0 %reduce-scatter.5.cloned.1.call-start = ((), (), s32[]{:S(2)}) async-start(), calls=%async_computation.3 | async-start | bytes 2359296 | tf_op jit(solution)/shard_map/reduce_scatter | solution.py:89
  90.1 47.0 %copy-start.13 = (bf16[256,256]{1,0:T(8,128)(2,1)S(1)}, bf16[256,256]{1,0:T(8,128)(2,1)}, u32[]{:S(2)}) copy-start(bf16[256,256]{1,0:T(8,128)(2,1)} %param.14) | copy-start | bytes 393220
  90.1 47.0 %copy-start.15 = (bf16[64,256]{1,0:T(8,128)(2,1)S(1)}, bf16[64,256]{1,0:T(8,128)(2,1)}, u32[]{:S(2)}) copy-start(bf16[64,256]{1,0:T(8,128)(2,1)} %copy-done.14) | copy-start | bytes 98308
  90.1 48.0 %copy-start.12 = (bf16[64,256]{1,0:T(8,128)(2,1)S(1)}, bf16[64,256]{1,0:T(8,128)(2,1)}, u32[]{:S(2)}) copy-start(bf16[64,256]{1,0:T(8,128)(2,1)} %copy-done.11) | copy-start | bytes 98308
  90.1 50.7 %copy-start.10 = (bf16[256,256]{1,0:T(8,128)(2,1)S(1)}, bf16[256,256]{1,0:T(8,128)(2,1)}, u32[]{:S(2)}) copy-start(bf16[256,256]{1,0:T(8,128)(2,1)} %param.13) | copy-start | bytes 393220
  90.1 101.0 %copy-start.18 = (bf16[256,256]{1,0:T(8,128)(2,1)S(1)}, bf16[256,256]{1,0:T(8,128)(2,1)}, u32[]{:S(2)}) copy-start(bf16[256,256]{1,0:T(8,128)(2,1)} %param.17) | copy-start | bytes 393220
  90.1 104.2 %copy-start.20 = (bf16[256,256]{1,0:T(8,128)(2,1)S(1)}, bf16[256,256]{1,0:T(8,128)(2,1)}, u32[]{:S(2)}) copy-start(bf16[256,256]{1,0:T(8,128)(2,1)} %param.16) | copy-start | bytes 393220
  90.1 263.7 %all-reduce.3.cloned.1.call-start = ((), (), s32[]{:S(2)}) async-start(), calls=%async_computation.4 | async-start | bytes 4718592 | tf_op jit(solution)/shard_map/psum | solution.py:98
  353.8 9.0 %copy-start.16 = (f32[256,256]{1,0:T(8,128)S(1)}, f32[256,256]{1,0:T(8,128)}, u32[]{:S(2)}) copy-start(f32[256,256]{1,0:T(8,128)} %get-tuple-element.28) | copy-start | bytes 786436
Sparse Core Ops, SparseCore 0:
  76.1 60.8 reduce-scatter.2
  139.6 51.4 reduce-scatter.4
  198.6 155.0 all-reduce.2
where the time goes:
time: 372 us; the launch traced here: 371 us
  waiting for transfers between devices  181 us (49%)
  blocking collectives  95 us (26%)
  matrix products  49.7 us (13%)
  local copies, waits for them, and re-layouts  18 us (5%)
  between operations  15.8 us (4%)
  other arithmetic  11.7 us (3%)
    psum x1, waiting for transfers between devices, on_device(): lax.psum((part_w_in, part_w_mid, part_w_out, part_v_in, part_v_mid, part_...  87.9 us
    psum x1, blocking collectives, on_device(): lax.psum((part_w_in, part_w_mid, part_w_out, part_v_in, part_v_mid, part_...  66.7 us
    reduce_scatter x1, waiting for transfers between devices, on_device(): lax.psum_scatter(basis_sum.astype(jnp.bfloat16), 'batch', scatter_dimensi...  48.8 us
    reduce_scatter x1, waiting for transfers between devices, on_device(): lax.psum_scatter(coeff_sum, 'grid', scatter_dimension=0, tiled=True)  43.7 us
    all_gather x1, blocking collectives, on_device(): shard_rows = lax.all_gather(coeff_own, 'grid', axis=0, tiled=True)  28.3 us
    dot_general x7, matrix products, contract_rows(): lax.dot_general(left_side, right_side, (((0,), (0,)), ((), ())), preferre...  24.1 us
    unnamed x48, local copies, waits for them, and re-layouts  18 us
    dot_general x3, matrix products, contract_cols(): lax.dot_general(left_side, right_side, (((1,), (1,)), ((), ())), preferre...  10.9 us
  transfers between devices with their start and end apart: 3, of which 3 were waited for; matrix products, arithmetic and copies ran while one was open for 6% of the time, Pallas kernels for 0%

commit v1 on v0

v1 whole, which is shorter than its diff:
```python
import functools
import math

import jax
import jax.numpy as jnp
from jax import lax
from jax.experimental import pallas as pl
from jax.experimental.pallas import tpu as pltpu
from jax.sharding import PartitionSpec as P

MESH = pl.DeviceIdType.MESH
BF = jnp.bfloat16
F32 = jnp.float32

GRID_SIDE = 8192
S0, S1, S2, S3 = 6.283164044266556, -41.33714236534519, 81.34076866645029, -70.99343091074333
ROUNDER = 12582912.0

PLANE = 16
LINE = 4
BRANCH_ROWS = 64
TRUNK_ROWS = 32


def dot(left, right, left_dim, right_dim):
    return lax.dot_general(
        left, right, (((left_dim,), (right_dim,)), ((), ())), preferred_element_type=F32
    )


def wave(phase):
    turn = phase - ((phase + ROUNDER) - ROUNDER)
    y = 0.25 - jnp.abs(turn)
    sq = y * y
    return y * (S0 + sq * (S1 + sq * (S2 + sq * S3)))


def coords():
    b = lax.axis_index("batch")
    g = lax.axis_index("grid")
    return b // 2, g // 4, ((g // 2) % 2) * 2 + b % 2, g % 2


def device(x, y, z, core):
    return {"batch": x * 2 + z % 2, "grid": y * 4 + (z // 2) * 2 + core}


def remote(src, dst, sems, k, target):
    return pltpu.make_async_remote_copy(
        src_ref=src,
        dst_ref=dst,
        send_sem=sems.at[0, k],
        recv_sem=sems.at[1, k],
        device_id=target,
        device_id_type=MESH,
    )


def wait_bytes(ref, sem):
    pltpu.make_async_copy(ref, ref, sem).wait()


class Reducer:
    def __init__(self, own, pair, send, recv, line, gathered, sems, rows, out_rows, has_loss):
        self.own, self.pair, self.send, self.recv = own, pair, send, recv
        self.line, self.gathered, self.sems = line, gathered, sems
        self.rows, self.out_rows, self.has_loss = rows, out_rows, has_loss
        self.x, self.y, self.z, self.core = coords()
        self.rank = self.y * 4 + self.z

    def peer(self, offset):
        t = (self.rank + offset) % PLANE
        return t, device(self.x, t // 4, t % 4, self.core)

    def sibling(self):
        return device(self.x, self.y, self.z, 1 - self.core)

    def start_pair(self):
        remote(self.own.at[1 - self.core], self.pair, self.sems, 0, self.sibling()).start()

    def start_plane(self):
        wait_bytes(self.pair, self.sems.at[1, 0])
        for m in range(PLANE):
            both = self.own[self.core, m] + self.pair[m]
            self.send[m] = both.astype(BF)
            if self.has_loss:
                square = both[48:56]
                high = square.astype(BF).astype(F32)
                self.send[m, 48:64] = jnp.concatenate([high, square - high], axis=0).astype(BF)
        self.recv[self.rank] = self.send[self.rank]

        @pl.loop(1, PLANE, unroll=True)
        def _(offset):
            t, target = self.peer(offset)
            remote(self.send.at[t], self.recv.at[self.rank], self.sems, 1, target).start()

    def start_line(self):
        wait_bytes(self.recv.at[pl.ds(0, PLANE - 1)], self.sems.at[1, 1])
        total = self.recv[0].astype(F32)
        for m in range(1, PLANE):
            total = total + self.recv[m].astype(F32)
        self.line[self.x] = total
        for offset in range(1, LINE):
            target = device((self.x + offset) % LINE, self.y, self.z, self.core)
            slot = self.line.at[self.x]
            remote(slot, slot, self.sems, 2, target).start()

    def start_gather(self):
        wait_bytes(self.line.at[pl.ds(0, LINE - 1)], self.sems.at[1, 2])
        total = (self.line[0] + self.line[1]) + (self.line[2] + self.line[3])
        self.gathered[self.core, self.rank] = total[: self.out_rows].astype(BF)
        slot = self.gathered.at[self.core, self.rank]

        @pl.loop(1, PLANE, unroll=True)
        def _(offset):
            _, target = self.peer(offset)
            remote(slot, slot, self.sems, 3, target).start()

        return total

    def start_return(self):
        half = self.gathered.at[self.core]
        wait_bytes(half.at[pl.ds(0, PLANE - 1)], self.sems.at[1, 3])
        remote(half, half, self.sems, 4, self.sibling()).start()

    def finish(self):
        wait_bytes(self.gathered.at[0], self.sems.at[1, 4])
        wait_bytes(self.pair, self.sems.at[0, 0])
        wait_bytes(self.send.at[pl.ds(0, PLANE - 1)], self.sems.at[0, 1])
        wait_bytes(self.line.at[pl.ds(0, LINE - 1)], self.sems.at[0, 2])
        wait_bytes(self.gathered.at[0, pl.ds(0, PLANE - 1)], self.sems.at[0, 3])
        wait_bytes(self.gathered.at[0], self.sems.at[0, 4])


def step_kernel(
    grad_factor,
    samples_in, index_in, targets_in, w_in_in, w_mid_in, w_out_in, v_in_in, v_mid_in, v_out_in,
    branch_out, trunk_out, loss_out,
    samples, index, targets, w_in, w_mid, w_out, v_in, v_mid, v_out,
    feats, t_one, t_two, basis, basis_grad, b_one, b_two, coeff, coeff_t, coeff_grad,
    squares,
    branch_own, branch_pair, branch_send, branch_recv, branch_line,
    trunk_own, trunk_pair, trunk_send, trunk_recv, trunk_line,
    local_sems, target_sems, branch_sems, trunk_sems,
):
    samp, pts = targets.shape
    chunks = target_sems.shape[0]
    chunk = samp // chunks
    x, y, z, core = coords()
    rank = y * 4 + z

    loads = []
    for k, (src, dst) in enumerate(
        (
            (index_in, index), (v_in_in, v_in), (v_mid_in, v_mid), (v_out_in, v_out),
            (w_in_in, w_in), (w_mid_in, w_mid), (w_out_in, w_out), (samples_in, samples),
        )
    ):
        copy = pltpu.make_async_copy(src, dst, local_sems.at[k])
        copy.start()
        loads.append(copy)
    target_loads = []
    for k in range(chunks):
        rows = pl.ds(k * chunk, chunk)
        copy = pltpu.make_async_copy(targets_in.at[rows], targets.at[rows], target_sems.at[k])
        copy.start()
        target_loads.append(copy)

    barrier = pltpu.get_barrier_semaphore()

    def greet(target):
        pl.semaphore_signal(barrier, inc=1, device_id=target, device_id_type=MESH)

    greet(device(x, y, z, 1 - core))
    for offset in range(1, LINE):
        greet(device((x + offset) % LINE, y, z, core))

    @pl.loop(1, PLANE)
    def _(offset):
        t = (rank + offset) % PLANE
        greet(device(x, t // 4, t % 4, core))

    for k in range(4):
        loads[k].wait()
    quarter = feats.shape[0] // 4
    order = lax.broadcasted_iota(jnp.int32, (quarter, 1), 0).astype(F32) + 1.0
    v_in_t, v_mid_t, v_out_t = v_in[...].T, v_mid[...].T, v_out[...].T
    wide = 1024
    for p in range(0, pts, wide):
        cols = pl.ds(p, wide)
        for axis in range(2):
            spot = index[axis : axis + 1, cols].astype(F32)
            phase = order * ((2.0 * spot + 1.0) * (0.25 / GRID_SIDE))
            base = 2 * axis * quarter
            feats[base : base + quarter, cols] = wave(phase - 0.25).astype(BF)
            feats[base + quarter : base + 2 * quarter, cols] = wave(phase).astype(BF)
        t_one[:, cols] = jnp.tanh(dot(v_in_t, feats[:, cols], 1, 0)).astype(BF)
        t_two[:, cols] = jnp.tanh(dot(v_mid_t, t_one[:, cols], 1, 0)).astype(BF)
        basis[:, cols] = dot(v_out_t, t_two[:, cols], 1, 0).astype(BF)

    for k in range(4, 8):
        loads[k].wait()
    b_one[...] = jnp.tanh(dot(samples[...], w_in[...], 1, 0)).astype(BF)
    b_two[...] = jnp.tanh(dot(b_one[...], w_mid[...], 1, 0)).astype(BF)
    coeff[...] = dot(b_two[...], w_out[...], 1, 0).astype(BF)
    coeff_t[...] = coeff[...].T

    squares[...] = jnp.zeros_like(squares)
    for k in range(chunks):
        rows = pl.ds(k * chunk, chunk)
        target_loads[k].wait()
        scaled = coeff[rows, :] * jnp.asarray(1.0 / 16.0, BF)
        for p in range(0, pts, wide):
            cols = pl.ds(p, wide)
            residual = dot(scaled, basis[:, cols], 1, 0) - targets[rows, cols].astype(F32)
            targets[rows, cols] = (residual * grad_factor).astype(BF)
            square = residual * residual
            squares[...] += jnp.sum(square.reshape(chunk // 8, 8, wide), axis=0)
        coeff_grad[rows, :] = dot(targets[rows, :], basis[...], 1, 1).astype(BF)

    grad = coeff_grad[...]
    part_out = dot(b_two[...], grad, 0, 0)
    slope = 1.0 - jnp.square(b_two[...].astype(F32))
    back_two = (dot(grad, w_out[...], 1, 1) * slope).astype(BF)
    part_mid = dot(b_one[...], back_two, 0, 0)
    slope = 1.0 - jnp.square(b_one[...].astype(F32))
    back_one = (dot(back_two, w_mid[...], 1, 1) * slope).astype(BF)
    part_in = dot(samples[...], back_one, 0, 0)
    square = jnp.sum(squares[...].reshape(8, wide // 128, 128), axis=1)
    square = jnp.concatenate([square, jnp.zeros_like(square)], axis=1)
    for m in range(2 * PLANE):
        c, r = m // PLANE, m % PLANE
        branch_own[c, r, 0:32] = part_in[m * 32 : m * 32 + 32]
        branch_own[c, r, 32:40] = part_mid[m * 8 : m * 8 + 8]
        branch_own[c, r, 40:48] = part_out[m * 8 : m * 8 + 8]
        branch_own[c, r, 48:56] = square
        branch_own[c, r, 56:64] = jnp.zeros_like(square)

    branch = Reducer(
        branch_own, branch_pair, branch_send, branch_recv, branch_line, branch_out,
        branch_sems, BRANCH_ROWS, 48, True,
    )
    trunk = Reducer(
        trunk_own, trunk_pair, trunk_send, trunk_recv, trunk_line, trunk_out,
        trunk_sems, TRUNK_ROWS, 32, False,
    )

    pl.semaphore_wait(barrier, PLANE + LINE - 1)
    branch.start_pair()

    def basis_columns(p):
        cols = pl.ds(p, wide)
        basis_grad[:, cols] = dot(coeff_t[...], targets[:, cols], 1, 0).astype(BF)

    for p in range(0, pts // 2, wide):
        basis_columns(p)
    branch.start_plane()
    for p in range(pts // 2, pts, wide):
        basis_columns(p)

    for p in range(0, pts, wide):
        cols = pl.ds(p, wide)
        grad = basis_grad[:, cols]
        last = dot(t_two[:, cols], grad, 1, 1)
        slope = 1.0 - jnp.square(t_two[:, cols].astype(F32))
        back_two = (dot(v_out[...], grad, 1, 0) * slope).astype(BF)
        middle = dot(t_one[:, cols], back_two, 1, 1)
        slope = 1.0 - jnp.square(t_one[:, cols].astype(F32))
        back_one = (dot(v_mid[...], back_two, 1, 0) * slope).astype(BF)
        first = dot(feats[:, cols], back_one, 1, 1)
        if p == 0:
            part_first, part_middle, part_last = first, middle, last
        else:
            part_first, part_middle, part_last = (
                part_first + first, part_middle + middle, part_last + last,
            )
    for m in range(2 * PLANE):
        c, r = m // PLANE, m % PLANE
        trunk_own[c, r, 0:8] = part_first[m * 8 : m * 8 + 8]
        trunk_own[c, r, 8:16] = part_middle[m * 8 : m * 8 + 8]
        trunk_own[c, r, 16:24] = part_last[m * 8 : m * 8 + 8]
        trunk_own[c, r, 24:32] = jnp.zeros((8, 256), F32)
    trunk.start_pair()
    branch.start_line()
    trunk.start_plane()
    square = branch.start_gather()[48:64]
    square = square[0:8] + square[8:16]
    loss_out[...] = jnp.sum(square, keepdims=True)
    trunk.start_line()
    trunk.start_gather()
    branch.start_return()
    trunk.start_return()
    branch.finish()
    trunk.finish()


def spread_kernel(
    loss_scale, branch, trunk, square, g_w_in, g_w_mid, g_w_out, g_v_in, g_v_mid, g_v_out, loss
):
    for m in range(2 * PLANE):
        c, r = m // PLANE, m % PLANE
        part = branch[c, r].astype(F32)
        g_w_in[m * 32 : m * 32 + 32] = part[0:32]
        g_w_mid[m * 8 : m * 8 + 8] = part[32:40]
        g_w_out[m * 8 : m * 8 + 8] = part[40:48]
        part = trunk[c, r].astype(F32)
        g_v_in[m * 8 : m * 8 + 8] = part[0:8]
        g_v_mid[m * 8 : m * 8 + 8] = part[8:16]
        g_v_out[m * 8 : m * 8 + 8] = part[16:24]
    loss[...] = square[...] * loss_scale


def on_device(samples, point_index, targets, w_in, w_mid, w_out, v_in, v_mid, v_out):
    samp, pts = targets.shape
    total_cells = samp * lax.axis_size("batch") * pts * lax.axis_size("grid")
    sensors, hidden = w_in.shape
    grad_factor = 64.0 / math.sqrt(total_cells) * w_out.shape[1] ** (-0.5)
    chunks = 4
    any_spec = pl.BlockSpec(memory_space=pl.ANY)
    vmem = pl.BlockSpec(memory_space=pltpu.VMEM)
    inputs = (samples, point_index, targets, w_in, w_mid, w_out, v_in, v_mid, v_out)
    v = pltpu.VMEM
    scratch = [v(a.shape, a.dtype) for a in inputs]
    scratch += [v((hidden, pts), BF)] * 5
    scratch += [v((samp, hidden), BF)] * 3 + [v((hidden, samp), BF), v((samp, hidden), BF)]
    scratch += [v((8, 1024), F32)]
    for rows in (BRANCH_ROWS, TRUNK_ROWS):
        scratch += [
            v((2, PLANE, rows, 256), F32),
            v((PLANE, rows, 256), F32),
            v((PLANE, rows, 256), BF),
            v((PLANE, rows, 256), BF),
            v((LINE, rows, 256), F32),
        ]
    scratch += [
        pltpu.SemaphoreType.DMA((8,)),
        pltpu.SemaphoreType.DMA((chunks,)),
        pltpu.SemaphoreType.DMA((2, 5)),
        pltpu.SemaphoreType.DMA((2, 5)),
    ]
    branch, trunk, square = pl.pallas_call(
        functools.partial(step_kernel, grad_factor),
        out_shape=(
            jax.ShapeDtypeStruct((2, PLANE, 48, 256), BF),
            jax.ShapeDtypeStruct((2, PLANE, TRUNK_ROWS, 256), BF),
            jax.ShapeDtypeStruct((1, 1), F32),
        ),
        in_specs=[any_spec] * 9,
        out_specs=[vmem] * 3,
        scratch_shapes=scratch,
        compiler_params=pltpu.CompilerParams(
            collective_id=0, has_side_effects=True, vmem_limit_bytes=58 << 20
        ),
        name="deeponet_step",
    )(*inputs)
    shapes = [(sensors, hidden)] + [(hidden, hidden)] * 5 + [(1, 1)]
    outs = pl.pallas_call(
        functools.partial(spread_kernel, 1.0 / (2.0 * total_cells)),
        out_shape=[jax.ShapeDtypeStruct(s, F32) for s in shapes],
        in_specs=[vmem] * 3,
        out_specs=[vmem] * 7,
        compiler_params=pltpu.CompilerParams(vmem_limit_bytes=32 << 20),
        name="spread_gradients",
    )(branch, trunk, square)
    return (*outs[:6], outs[6].reshape(()))


def solution(mesh):
    placed = (P("batch", None), P(None, "grid"), P("batch", "grid"), P(), P(), P(), P(), P(), P())
    return jax.shard_map(
        on_device,
        mesh=mesh,
        in_specs=placed,
        out_specs=(P(), P(), P(), P(), P(), P(), P()),
        check_vma=False,
    )
```

time: 372 us -> 56 us (0.15)
  waiting for transfers between devices: 181 us -> 0 us
  blocking collectives: 95 us -> 0 us
  Pallas kernels: 0 us -> 53 us
  matrix products: 49.7 us -> 0 us
  local copies, waits for them, and re-layouts: 18 us -> 2.17 us
  between operations: 15.8 us -> 0.65 us
  other arithmetic: 11.7 us -> 0 us
    reduce_scatter x2 -> x0, waiting for transfers between devices: 92.6 us -> none  [the longest x1 48.8 us: on_device(): lax.psum_scatter(basis_sum.astype(jnp.bfloat16), 'batch', scatter_dimensi...]
    psum x1 -> x0, waiting for transfers between devices: 87.9 us -> none  [on_device(): lax.psum((part_w_in, part_w_mid, part_w_out, part_v_in, part_v_mid, part_...]
    psum x1 -> x0, blocking collectives: 66.7 us -> none  [on_device(): lax.psum((part_w_in, part_w_mid, part_w_out, part_v_in, part_v_mid, part_...]
    pallas_call x0 -> x2, Pallas kernels: none -> 53 us  [the longest x1 50.9 us: on_device(): pl.pallas_call(functools.partial(step_kernel, grad_factor), out_shape=(ja...]
    dot_general x17 -> x0, matrix products: 49.7 us -> none  [the longest x7 24.1 us: contract_rows(): lax.dot_general(left_side, right_side, (((0,), (0,)), ((), ())), preferre...]
    all_gather x1 -> x0, blocking collectives: 28.3 us -> none  [on_device(): shard_rows = lax.all_gather(coeff_own, 'grid', axis=0, tiled=True)]
    unnamed x48 -> x4, local copies, waits for them, and re-layouts: 18 us -> 2.17 us
    another operation x1 -> x0, other arithmetic: 7.66 us -> none
  transfers between devices with their start and end apart: 3 -> 0, of which waited for: 3 -> 0; matrix products, arithmetic and copies ran while one was open for 6% -> 0% of each run, Pallas kernels for 0% -> 0%
where the time goes in v1:
time: 56 us; the launch traced here: 55.8 us
  Pallas kernels  53 us (95%)
  local copies, waits for them, and re-layouts  2.17 us (4%)
  between operations  0.65 us (1%)
    pallas_call x1, Pallas kernels, on_device(): pl.pallas_call(functools.partial(step_kernel, grad_factor), out_shape=(ja...  50.9 us
    unnamed x4, local copies, waits for them, and re-layouts  2.17 us
    pallas_call x1, Pallas kernels, on_device(): pl.pallas_call(functools.partial(spread_kernel, 1.0 / (2.0 * total_cells)...  2.08 us

profile of v1, /device:TPU:1, one launch (start us, length us, event | category | flops | bytes accessed | tf_op | source)
XLA Modules:
  0.0 55.8 jit_solution(14358894635458710493)
XLA Ops:
  0.6 50.9 %deeponet_step.1 = (bf16[2,16,48,256]{3,2,1,0:T(8,128)(2,1)}, bf16[2,16,32,256]{3,2,1,0:T(8,128)(2,1)}, f32[1,1]{1,0:T(1,128)}) custom-call(bf16[1024,1024]{1,0:T(8,128)(2,1)} %samples_in.1, s32[2,4096]{1,0:T(2,128)} %index_in.1, bf16[1024,4096]{1,0:T(8,128)(2,1)} %targets_in.1, bf16[1024,256]{1,0:T(8,128)(2,1)} %w_in_in.1, bf16[256,256]{1,0:T(8,128)(2,1)} %w_mid_in.1, ...), custom_call_target="tpu_custom_call" | custom-call | tf_op jit(solution)/shard_map/deeponet_step/pallas_call | solution.py:341
  51.6 0.0 copy-start
  51.6 1.1 %copy-done = bf16[2,16,48,256]{3,2,1,0:T(8,128)(2,1)S(1)} copy-done((bf16[2,16,48,256]{3,2,1,0:T(8,128)(2,1)S(1)}, bf16[2,16,48,256]{3,2,1,0:T(8,128)(2,1)}, u32[]{:S(2)}) %copy-start) | copy-done | bytes 786456
  52.7 0.0 copy-start.1
  52.7 1.0 %copy-done.1 = bf16[2,16,32,256]{3,2,1,0:T(8,128)(2,1)S(1)} copy-done((bf16[2,16,32,256]{3,2,1,0:T(8,128)(2,1)S(1)}, bf16[2,16,32,256]{3,2,1,0:T(8,128)(2,1)}, u32[]{:S(2)}) %copy-start.1) | copy-done | bytes 524312
  53.7 2.1 %spread_gradients.1 = (f32[1024,256]{1,0:T(8,128)}, f32[256,256]{1,0:T(8,128)}, f32[256,256]{1,0:T(8,128)}, f32[256,256]{1,0:T(8,128)}, f32[256,256]{1,0:T(8,128)}, /*index=5*/f32[256,256]{1,0:T(8,128)}, f32[1,1]{1,0:T(1,128)}) custom-call(bf16[2,16,48,256]{3,2,1,0:T(8,128)(2,1)S(1)} %copy-done, bf16[2,16,32,256]{3,2,1,0:T(8,128)(2,1)S(1)} %copy-done.1, ...), custom_call_target="tpu_custom_call" | custom-call | tf_op jit(solution)/shard_map/spread_gradients/pallas_call | solution.py:357
Async XLA Ops:
  51.6 1.1 %copy-start = (bf16[2,16,48,256]{3,2,1,0:T(8,128)(2,1)S(1)}, bf16[2,16,48,256]{3,2,1,0:T(8,128)(2,1)}, u32[]{:S(2)}) copy-start(bf16[2,16,48,256]{3,2,1,0:T(8,128)(2,1)} %get-tuple-element.17.branch) | copy-start | bytes 2359300
  52.7 1.0 %copy-start.1 = (bf16[2,16,32,256]{3,2,1,0:T(8,128)(2,1)S(1)}, bf16[2,16,32,256]{3,2,1,0:T(8,128)(2,1)}, u32[]{:S(2)}) copy-start(bf16[2,16,32,256]{3,2,1,0:T(8,128)(2,1)} %get-tuple-element.18.trunk) | copy-start | bytes 1572868

commit v2 on v1

v2 whole, which is shorter than its diff:
```python
import functools
import itertools
import math

import jax
import jax.numpy as jnp
from jax import lax
from jax.experimental import pallas as pl
from jax.experimental.pallas import tpu as pltpu
from jax.sharding import PartitionSpec as P

MESH = pl.DeviceIdType.MESH
BF = jnp.bfloat16
F32 = jnp.float32

GRID_SIDE = 8192
S0, S1, S2, S3, S4 = (
    6.283185160089221, -41.34165503135105, 81.60100406887733, -76.54978218664795, 39.536705209824365,
)
ROUNDER = 12582912.0

CHIPS = 64
TILE = (16, 128)
BRANCH_TILES, TRUNK_TILES = 96, 64
LOSS_TILE = 48


def dot(left, right, left_dim, right_dim):
    return lax.dot_general(
        left, right, (((left_dim,), (right_dim,)), ((), ())), preferred_element_type=F32
    )


def wave(phase):
    turn = phase - ((phase + ROUNDER) - ROUNDER)
    y = 0.25 - jnp.abs(turn)
    sq = y * y
    return y * (S0 + sq * (S1 + sq * (S2 + sq * (S3 + sq * S4))))


def waves(turns, count):
    order = lax.broadcasted_iota(jnp.int32, (8, 1), 0).astype(F32) + 1.0
    phase = order * turns
    sines, cosines = [wave(phase - 0.25)], [wave(phase)]
    while len(sines) * 8 < count:
        by_sin, by_cos = sines[-1][7:8], cosines[-1][7:8]
        pairs = list(zip(sines, cosines))
        sines += [s * by_cos + c * by_sin for s, c in pairs]
        cosines += [c * by_cos - s * by_sin for s, c in pairs]
    return jnp.concatenate(sines, axis=0), jnp.concatenate(cosines, axis=0)


def halves(square):
    high = square.astype(BF).astype(F32)
    return jnp.concatenate([high, square - high], axis=0).astype(BF)


def coords():
    b = lax.axis_index("batch")
    g = lax.axis_index("grid")
    return b // 2, g // 4, ((g // 2) % 2) * 2 + b % 2, g % 2


def device(x, y, z, core):
    return {"batch": x * 2 + z % 2, "grid": y * 4 + (z // 2) * 2 + core}


def remote(src, dst, sems, k, target):
    return pltpu.make_async_remote_copy(
        src_ref=src,
        dst_ref=dst,
        send_sem=sems.at[0, k],
        recv_sem=sems.at[1, k],
        device_id=target,
        device_id_type=MESH,
    )


def wait_bytes(ref, sem):
    pltpu.make_async_copy(ref, ref, sem).wait()


OFFSETS = sorted(
    (o for o in itertools.product(range(4), repeat=3) if any(o)),
    key=lambda o: -sum(min(d, 4 - d) for d in o),
)


def chip_tiles(rank, doubled):
    if not doubled:
        return rank, 1
    even = (rank // 16 + rank // 4 + rank) % 2 == 0
    return 3 * (rank // 2) + (rank % 2) * (1 if even else 2), 2 if even else 1


class Reducer:
    def __init__(self, own, pair_send, pair_recv, send, recv, result, gathered, sems, doubled):
        self.own, self.pair_send, self.pair_recv = own, pair_send, pair_recv
        self.send, self.recv, self.result, self.gathered = send, recv, result, gathered
        self.sems, self.doubled = sems, doubled
        self.tiles = own.shape[1]
        self.x, self.y, self.z, self.core = coords()
        self.rank = (self.x * 4 + self.y) * 4 + self.z
        self.odd = (self.x + self.y + self.z) % 2
        xs = [(self.x + d) % 4 for d in range(4)]
        ys = [(self.y + d) % 4 for d in range(4)]
        zs = [(self.z + d) % 4 for d in range(4)]
        ranks = [x * 16 for x in xs], [y * 4 for y in ys], zs
        batches = [x * 2 for x in xs], [z % 2 for z in zs]
        grids = [y * 4 + self.core for y in ys], [(z // 2) * 2 for z in zs]
        self.others = [
            (
                sum(o) % 2,
                ranks[0][o[0]] + ranks[1][o[1]] + ranks[2][o[2]],
                {"batch": batches[0][o[0]] + batches[1][o[2]], "grid": grids[0][o[1]] + grids[1][o[2]]},
            )
            for o in OFFSETS
        ]

    def by_parity(self, action):
        if self.doubled:
            pl.when(self.odd == 0)(lambda: action(0))
            pl.when(self.odd == 1)(lambda: action(1))
        else:
            action(0)

    def place(self, rank, odd):
        if not self.doubled:
            return rank, 1
        return 3 * (rank // 2) + (rank % 2) * (1 + odd), 2 - odd

    def sibling(self):
        return device(self.x, self.y, self.z, 1 - self.core)

    def start_pair(self, square=None):
        self.pair_send[...] = self.own[1 - self.core].astype(BF)
        if square is not None:
            self.pair_send[LOSS_TILE] = halves(square)
        remote(self.pair_send, self.pair_recv, self.sems, 0, self.sibling()).start()

    def start_scatter(self, square=None):
        wait_bytes(self.pair_recv, self.sems.at[1, 0])
        self.send[...] = (self.own[self.core] + self.pair_recv[...].astype(F32)).astype(BF)
        if square is not None:
            both = self.pair_recv[LOSS_TILE].astype(F32)
            self.send[LOSS_TILE] = halves(square + (both[:8] + both[8:]))

        def go(odd):
            spot, count = self.place(self.rank, odd)
            for k in range(count):
                self.recv[k, self.rank] = self.send[spot + k]
            for turn, rank, target in self.others:
                spot, count = self.place(rank, (odd + turn) % 2)
                src = self.send.at[pl.ds(spot, count)]
                dst = self.recv.at[pl.ds(0, count), self.rank]
                remote(src, dst, self.sems, 1, target).start()

        self.by_parity(go)

    def start_gather(self, has_square=False):
        def go(odd):
            spot, count = self.place(self.rank, odd)
            wait_bytes(self.recv.at[pl.ds(0, count), pl.ds(0, CHIPS - 1)], self.sems.at[1, 1])
            for k in range(count):
                total = jnp.sum(self.recv[k].astype(F32), axis=0)
                sent = total.astype(BF)
                if has_square:
                    sent = jnp.where(self.rank == LOSS_TILE, halves(total[:8] + total[8:]), sent)
                self.result[k] = sent
            src = self.result.at[pl.ds(0, count)]
            dst = self.gathered.at[self.core, pl.ds(spot, count)]
            for _, _, target in self.others:
                remote(src, dst, self.sems, 3, target).start()
            pltpu.make_async_copy(src, dst, self.sems.at[0, 5]).start()

        self.by_parity(go)

    def start_return(self):
        half = self.gathered.at[self.core]

        def go(odd):
            spot, count = self.place(self.rank, odd)
            wait_bytes(self.result.at[pl.ds(0, count)], self.sems.at[0, 5])
            wait_bytes(self.send.at[pl.ds(0, self.tiles - count)], self.sems.at[1, 3])

        self.by_parity(go)
        remote(half, half, self.sems, 4, self.sibling()).start()

    def finish(self):
        wait_bytes(self.pair_send, self.sems.at[0, 0])

        def go(odd):
            _, count = self.place(self.rank, odd)
            wait_bytes(self.send.at[pl.ds(0, self.tiles - count)], self.sems.at[0, 1])
            wait_bytes(self.recv.at[pl.ds(0, count), pl.ds(0, CHIPS - 1)], self.sems.at[0, 3])

        self.by_parity(go)
        wait_bytes(self.pair_send, self.sems.at[0, 4])
        wait_bytes(self.pair_recv, self.sems.at[1, 4])


def tile_spots():
    places = [chip_tiles(r, True) for r in range(CHIPS)]
    return [s for s, _ in places], [s + 1 for s, n in places if n == 2]


def step_kernel(
    grad_factor,
    samples_in, index_in, targets_in, w_in_in, w_mid_in, w_out_in, v_in_in, v_mid_in, v_out_in,
    branch_out, trunk_out,
    samples, index, targets, w_in, w_mid, w_out, v_in, v_mid, v_out,
    feats, t_one, t_two, basis, basis_grad, b_one, b_two, coeff, coeff_t, coeff_grad,
    squares,
    branch_own, branch_pair_send, branch_pair_recv, branch_send, branch_recv, branch_result,
    trunk_own, trunk_pair_send, trunk_pair_recv, trunk_send, trunk_recv, trunk_result,
    local_sems, target_sems, branch_sems, trunk_sems,
):
    samp, pts = targets.shape
    chunks = target_sems.shape[0]
    chunk = samp // chunks
    branch = Reducer(
        branch_own, branch_pair_send, branch_pair_recv, branch_send, branch_recv, branch_result,
        branch_out, branch_sems, True,
    )
    trunk = Reducer(
        trunk_own, trunk_pair_send, trunk_pair_recv, trunk_send, trunk_recv, trunk_result,
        trunk_out, trunk_sems, False,
    )

    loads = []
    for k, (src, dst) in enumerate(
        (
            (index_in, index), (v_in_in, v_in), (v_mid_in, v_mid), (v_out_in, v_out),
            (w_in_in, w_in), (w_mid_in, w_mid), (w_out_in, w_out), (samples_in, samples),
        )
    ):
        copy = pltpu.make_async_copy(src, dst, local_sems.at[k])
        copy.start()
        loads.append(copy)
    target_loads = []
    for k in range(chunks):
        rows = pl.ds(k * chunk, chunk)
        copy = pltpu.make_async_copy(targets_in.at[rows], targets.at[rows], target_sems.at[k])
        copy.start()
        target_loads.append(copy)

    barrier = pltpu.get_barrier_semaphore()

    def greet(target):
        pl.semaphore_signal(barrier, inc=1, device_id=target, device_id_type=MESH)

    greet(trunk.sibling())
    for _, _, target in trunk.others:
        greet(target)

    for k in range(4):
        loads[k].wait()
    quarter = feats.shape[0] // 4
    v_in_t, v_mid_t, v_out_t = v_in[...].T, v_mid[...].T, v_out[...].T
    wide = 1024
    block = 512
    blocks = pts // block

    def trunk_feats(p):
        cols = pl.ds(p * block, block)
        for axis in range(2):
            turns = (2.0 * index[axis : axis + 1, cols].astype(F32) + 1.0) * (0.25 / GRID_SIDE)
            sines, cosines = waves(turns, quarter)
            base = 2 * axis * quarter
            feats[base : base + quarter, cols] = sines.astype(BF)
            feats[base + quarter : base + 2 * quarter, cols] = cosines.astype(BF)

    def trunk_one(p):
        cols = pl.ds(p * block, block)
        t_one[:, cols] = jnp.tanh(dot(v_in_t, feats[:, cols], 1, 0)).astype(BF)

    def trunk_two(p):
        cols = pl.ds(p * block, block)
        t_two[:, cols] = jnp.tanh(dot(v_mid_t, t_one[:, cols], 1, 0)).astype(BF)

    def trunk_basis(p):
        cols = pl.ds(p * block, block)
        basis[:, cols] = dot(v_out_t, t_two[:, cols], 1, 0).astype(BF)

    quarter_rows = samp // 4

    def branch_one(k):
        rows = pl.ds(k * quarter_rows, quarter_rows)
        b_one[rows, :] = jnp.tanh(dot(samples[rows, :], w_in[...], 1, 0)).astype(BF)

    def branch_two(k):
        rows = pl.ds(k * quarter_rows, quarter_rows)
        b_two[rows, :] = jnp.tanh(dot(b_one[rows, :], w_mid[...], 1, 0)).astype(BF)

    def branch_coeff(k):
        rows = pl.ds(k * quarter_rows, quarter_rows)
        coeff[rows, :] = dot(b_two[rows, :], w_out[...], 1, 0).astype(BF)

    stages = (trunk_feats, trunk_one, trunk_two, trunk_basis)
    branch_stages = (branch_one, branch_two, branch_coeff)
    branch_from = 5
    for step in range(blocks + len(stages) - 1):
        if step == branch_from:
            for k in range(4, 8):
                loads[k].wait()
        for lag, stage in enumerate(stages):
            if 0 <= step - lag < blocks:
                stage(step - lag)
        for lag, stage in enumerate(branch_stages):
            if 0 <= step - branch_from - lag < 4:
                stage(step - branch_from - lag)
    coeff_t[...] = coeff[...].T

    squares[...] = jnp.zeros_like(squares)
    for k in range(chunks):
        rows = pl.ds(k * chunk, chunk)
        target_loads[k].wait()
        scaled = coeff[rows, :] * jnp.asarray(1.0 / 16.0, BF)
        for p in range(0, pts, wide):
            cols = pl.ds(p, wide)
            residual = dot(scaled, basis[:, cols], 1, 0) - targets[rows, cols].astype(F32)
            targets[rows, cols] = (residual * grad_factor).astype(BF)
            square = residual * residual
            squares[...] += jnp.sum(square.reshape(chunk // 8, 8, wide), axis=0)
        coeff_grad[rows, :] = dot(targets[rows, :], basis[...], 1, 1).astype(BF)

    grad = coeff_grad[...]
    part_out = dot(b_two[...], grad, 0, 0)
    slope = 1.0 - jnp.square(b_two[...].astype(F32))
    back_two = (dot(grad, w_out[...], 1, 1) * slope).astype(BF)
    part_mid = dot(b_one[...], back_two, 0, 0)
    slope = 1.0 - jnp.square(b_one[...].astype(F32))
    back_one = (dot(back_two, w_mid[...], 1, 1) * slope).astype(BF)
    part_in = dot(samples[...], back_one, 0, 0)
    square = jnp.sum(squares[...].reshape(8, wide // 128, 128), axis=1)

    def pack(own, part, core, spots, row):
        for k, spot in enumerate(spots):
            strip = part[row + 8 * k : row + 8 * k + 8]
            own[core, spot, 0:8] = strip[:, :128]
            own[core, spot, 8:16] = strip[:, 128:]

    singles, doubles = tile_spots()
    for c in range(2):
        pack(branch_own, part_in, c, singles, c * 512)
        pack(branch_own, part_mid, c, doubles[:16], c * 128)
        pack(branch_own, part_out, c, doubles[16:], c * 128)

    pl.semaphore_wait(barrier, CHIPS)
    branch.start_pair()

    def basis_columns(p):
        cols = pl.ds(p, wide)
        basis_grad[:, cols] = dot(coeff_t[...], targets[:, cols], 1, 0).astype(BF)

    for p in range(0, pts // 2, wide):
        basis_columns(p)
    branch.start_scatter()
    for p in range(pts // 2, pts, wide):
        basis_columns(p)

    for p in range(0, pts, wide):
        cols = pl.ds(p, wide)
        grad = basis_grad[:, cols]
        last = dot(t_two[:, cols], grad, 1, 1)
        slope = 1.0 - jnp.square(t_two[:, cols].astype(F32))
        back_two = (dot(v_out[...], grad, 1, 0) * slope).astype(BF)
        middle = dot(t_one[:, cols], back_two, 1, 1)
        slope = 1.0 - jnp.square(t_one[:, cols].astype(F32))
        back_one = (dot(v_mid[...], back_two, 1, 0) * slope).astype(BF)
        first = dot(feats[:, cols], back_one, 1, 1)
        if p == 0:
            part_first, part_middle, part_last = first, middle, last
        else:
            part_first, part_middle, part_last = (
                part_first + first, part_middle + middle, part_last + last,
            )
    for c in range(2):
        for k, part in enumerate((part_first, part_middle, part_last)):
            pack(trunk_own, part, c, range(16 * k, 16 * k + 16), c * 128)
        trunk_own[c, LOSS_TILE:] = jnp.zeros((TRUNK_TILES - LOSS_TILE, *TILE), F32)
    trunk.start_pair(square)
    trunk.start_scatter(square)
    branch.start_gather()
    trunk.start_gather(has_square=True)
    branch.start_return()
    trunk.start_return()
    branch.finish()
    trunk.finish()


def spread_kernel(
    loss_scale, branch_in, trunk_in, g_w_in, g_w_mid, g_w_out, g_v_in, g_v_mid, g_v_out, loss,
    branch, trunk, w_in, w_mid, w_out, v_in, v_mid, v_out, in_sems, out_sems,
):
    pieces = [(trunk_in, trunk, 0), (trunk_in, trunk, 1), (branch_in, branch, 0), (branch_in, branch, 1)]
    loads = [
        pltpu.make_async_copy(src.at[c], dst.at[c], in_sems.at[k])
        for k, (src, dst, c) in enumerate(pieces)
    ]
    for load in loads:
        load.start()
    stores = []

    def put(src, c, spots, held, out):
        rows = 8 * len(spots)
        for k, spot in enumerate(spots):
            tile = src[c, spot].astype(F32)
            row = c * rows + 8 * k
            held[row : row + 8, 0:128] = tile[:8]
            held[row : row + 8, 128:256] = tile[8:]
        span = pl.ds(c * rows, rows)
        store = pltpu.make_async_copy(held.at[span], out.at[span], out_sems.at[len(stores)])
        store.start()
        stores.append(store)

    for c in range(2):
        loads[c].wait()
        for k, (held, out) in enumerate(((v_in, g_v_in), (v_mid, g_v_mid), (v_out, g_v_out))):
            put(trunk, c, range(16 * k, 16 * k + 16), held, out)
    singles, doubles = tile_spots()
    for c in range(2):
        loads[2 + c].wait()
        put(branch, c, singles, w_in, g_w_in)
        put(branch, c, doubles[:16], w_mid, g_w_mid)
        put(branch, c, doubles[16:], w_out, g_w_out)
    square = jnp.sum(trunk[0, LOSS_TILE].astype(F32), keepdims=True)
    loss[...] = square * loss_scale
    for store in stores:
        store.wait()


def on_device(samples, point_index, targets, w_in, w_mid, w_out, v_in, v_mid, v_out):
    samp, pts = targets.shape
    total_cells = samp * lax.axis_size("batch") * pts * lax.axis_size("grid")
    sensors, hidden = w_in.shape
    grad_factor = 64.0 / math.sqrt(total_cells) * w_out.shape[1] ** (-0.5)
    chunks = 4
    any_spec = pl.BlockSpec(memory_space=pl.ANY)
    vmem = pl.BlockSpec(memory_space=pltpu.VMEM)
    inputs = (samples, point_index, targets, w_in, w_mid, w_out, v_in, v_mid, v_out)
    v = pltpu.VMEM
    scratch = [v(a.shape, a.dtype) for a in inputs]
    scratch += [v((hidden, pts), BF)] * 5
    scratch += [v((samp, hidden), BF)] * 3 + [v((hidden, samp), BF), v((samp, hidden), BF)]
    scratch += [v((8, 1024), F32)]
    for tiles, most in ((BRANCH_TILES, 2), (TRUNK_TILES, 1)):
        scratch += [
            v((2, tiles, *TILE), F32),
            v((tiles, *TILE), BF),
            v((tiles, *TILE), BF),
            v((tiles, *TILE), BF),
            v((most, CHIPS, *TILE), BF),
            v((most, *TILE), BF),
        ]
    scratch += [
        pltpu.SemaphoreType.DMA((8,)),
        pltpu.SemaphoreType.DMA((chunks,)),
        pltpu.SemaphoreType.DMA((2, 6)),
        pltpu.SemaphoreType.DMA((2, 6)),
    ]
    branch, trunk = pl.pallas_call(
        functools.partial(step_kernel, grad_factor),
        out_shape=(
            jax.ShapeDtypeStruct((2, BRANCH_TILES, *TILE), BF),
            jax.ShapeDtypeStruct((2, TRUNK_TILES, *TILE), BF),
        ),
        in_specs=[any_spec] * 9,
        out_specs=[any_spec] * 2,
        scratch_shapes=scratch,
        compiler_params=pltpu.CompilerParams(
            collective_id=0, has_side_effects=True, vmem_limit_bytes=58 << 20
        ),
        name="deeponet_step",
    )(*inputs)
    shapes = [(sensors, hidden)] + [(hidden, hidden)] * 5 + [(1, 1)]
    outs = pl.pallas_call(
        functools.partial(spread_kernel, 1.0 / (2.0 * total_cells)),
        out_shape=[jax.ShapeDtypeStruct(s, F32) for s in shapes],
        in_specs=[any_spec] * 2,
        out_specs=[any_spec] * 6 + [vmem],
        scratch_shapes=[v((2, BRANCH_TILES, *TILE), BF), v((2, TRUNK_TILES, *TILE), BF)]
        + [v(s, F32) for s in shapes[:6]]
        + [pltpu.SemaphoreType.DMA((4,)), pltpu.SemaphoreType.DMA((12,))],
        compiler_params=pltpu.CompilerParams(vmem_limit_bytes=60 << 20),
        name="spread_gradients",
    )(branch, trunk)
    return (*outs[:6], outs[6].reshape(()))


def solution(mesh):
    placed = (P("batch", None), P(None, "grid"), P("batch", "grid"), P(), P(), P(), P(), P(), P())
    return jax.shard_map(
        on_device,
        mesh=mesh,
        in_specs=placed,
        out_specs=(P(), P(), P(), P(), P(), P(), P()),
        check_vma=False,
    )
```

time: 56 us -> 50.7 us (0.905)
  Pallas kernels: 53 us -> 49.8 us
  local copies, waits for them, and re-layouts: 2.17 us -> 0 us
    pallas_call x1, Pallas kernels: 50.9 us -> 46.8 us  [on_device(): pl.pallas_call(functools.partial(step_kernel, grad_factor), out_shape=(ja...]
    unnamed x4 -> x0, local copies, waits for them, and re-layouts: 2.17 us -> none
    pallas_call x1, Pallas kernels: 2.08 us -> 3 us  [on_device(): pl.pallas_call(functools.partial(spread_kernel, 1.0 / (2.0 * total_cells)...]
where the time goes in v2:
time: 50.7 us; the launch traced here: 50.6 us
  Pallas kernels  49.8 us (98%)
  between operations  0.8 us (2%)
    pallas_call x1, Pallas kernels, on_device(): pl.pallas_call(functools.partial(step_kernel, grad_factor), out_shape=(ja...  46.8 us
    pallas_call x1, Pallas kernels, on_device(): pl.pallas_call(functools.partial(spread_kernel, 1.0 / (2.0 * total_cells)...  3 us

profile of v2, /device:TPU:1, one launch (start us, length us, event | category | flops | bytes accessed | tf_op | source)
XLA Modules:
  0.0 50.6 jit_solution(6736268190939933580)
XLA Ops:
  0.6 46.8 %deeponet_step.1 = (bf16[2,96,16,128]{3,2,1,0:T(8,128)(2,1)}, bf16[2,64,16,128]{3,2,1,0:T(8,128)(2,1)}) custom-call(bf16[1024,1024]{1,0:T(8,128)(2,1)} %samples_in.1, s32[2,4096]{1,0:T(2,128)} %index_in.1, bf16[1024,4096]{1,0:T(8,128)(2,1)} %targets_in.1, bf16[1024,256]{1,0:T(8,128)(2,1)} %w_in_in.1, bf16[256,256]{1,0:T(8,128)(2,1)} %w_mid_in.1, ...), custom_call_target="tpu_custom_call" | custom-call | tf_op jit(solution)/shard_map/deeponet_step/pallas_call | solution.py:462
  47.5 3.0 %spread_gradients.1 = (f32[1024,256]{1,0:T(8,128)}, f32[256,256]{1,0:T(8,128)}, f32[256,256]{1,0:T(8,128)}, f32[256,256]{1,0:T(8,128)}, f32[256,256]{1,0:T(8,128)}, /*index=5*/f32[256,256]{1,0:T(8,128)}, f32[1,1]{1,0:T(1,128)}) custom-call(bf16[2,96,16,128]{3,2,1,0:T(8,128)(2,1)} %get-tuple-element.16.branch_in, ...), custom_call_target="tpu_custom_call" | custom-call | tf_op jit(solution)/shard_map/spread_gradients/pallas_call | solution.py:477

commit v3 on v2

v3 whole, which is shorter than its diff:
```python
import functools
import itertools
import math

import jax
import jax.numpy as jnp
from jax import lax
from jax.experimental import pallas as pl
from jax.experimental.pallas import tpu as pltpu
from jax.sharding import PartitionSpec as P

MESH = pl.DeviceIdType.MESH
BF = jnp.bfloat16
F32 = jnp.float32

GRID_SIDE = 8192
S0, S1, S2, S3, S4 = (
    6.283185160089221, -41.34165503135105, 81.60100406887733, -76.54978218664795, 39.536705209824365,
)
ROUNDER = 12582912.0

CHIPS = 64
TILE = (16, 128)
BRANCH_TILES, TRUNK_TILES, FIRST_TILES = 96, 32, 16


def dot(left, right, left_dim, right_dim):
    return lax.dot_general(
        left, right, (((left_dim,), (right_dim,)), ((), ())), preferred_element_type=F32
    )


def wave(phase):
    turn = phase - ((phase + ROUNDER) - ROUNDER)
    y = 0.25 - jnp.abs(turn)
    sq = y * y
    return y * (S0 + sq * (S1 + sq * (S2 + sq * (S3 + sq * S4))))


def waves(turns, count):
    order = lax.broadcasted_iota(jnp.int32, (8, 1), 0).astype(F32) + 1.0
    phase = order * turns
    sines, cosines = [wave(phase - 0.25)], [wave(phase)]
    while len(sines) * 8 < count:
        by_sin, by_cos = sines[-1][7:8], cosines[-1][7:8]
        pairs = list(zip(sines, cosines))
        sines += [s * by_cos + c * by_sin for s, c in pairs]
        cosines += [c * by_cos - s * by_sin for s, c in pairs]
    return jnp.concatenate(sines, axis=0), jnp.concatenate(cosines, axis=0)


def coords():
    b = lax.axis_index("batch")
    g = lax.axis_index("grid")
    return b // 2, g // 4, ((g // 2) % 2) * 2 + b % 2, g % 2


def device(x, y, z, core):
    return {"batch": x * 2 + z % 2, "grid": y * 4 + (z // 2) * 2 + core}


def remote(src, dst, sems, k, target):
    return pltpu.make_async_remote_copy(
        src_ref=src,
        dst_ref=dst,
        send_sem=sems.at[0, k],
        recv_sem=sems.at[1, k],
        device_id=target,
        device_id_type=MESH,
    )


def wait_bytes(ref, sem):
    pltpu.make_async_copy(ref, ref, sem).wait()


OFFSETS = sorted(
    itertools.product(range(4), repeat=3), key=lambda o: -sum(min(d, 4 - d) for d in o)
)


def chip_tiles(rank):
    even = (rank // 16 + rank // 4 + rank) % 2 == 0
    return 3 * (rank // 2) + (rank % 2) * (1 if even else 2), 2 if even else 1


class Chips:
    def __init__(self):
        self.x, self.y, self.z, self.core = coords()
        self.rank = (self.x * 4 + self.y) * 4 + self.z
        self.odd = (self.x + self.y + self.z) % 2
        self.sibling = device(self.x, self.y, self.z, 1 - self.core)
        xs = [(self.x + d) % 4 for d in range(4)]
        ys = [(self.y + d) % 4 for d in range(4)]
        zs = [(self.z + d) % 4 for d in range(4)]
        ranks = [x * 16 for x in xs], [y * 4 for y in ys], zs
        batches = [x * 2 for x in xs], [z % 2 for z in zs]
        grids = [y * 4 + self.core for y in ys], [(z // 2) * 2 for z in zs]
        self.all = [
            (
                sum(o),
                ranks[0][o[0]] + ranks[1][o[1]] + ranks[2][o[2]],
                {"batch": batches[0][o[0]] + batches[1][o[2]], "grid": grids[0][o[1]] + grids[1][o[2]]},
            )
            for o in OFFSETS
        ]
        self.others = self.all[:-1]


class Reducer:
    def __init__(self, chips, own, pair_send, pair_recv, send, recv, half, out, sems, counts):
        self.chips = chips
        self.own, self.pair_send, self.pair_recv = own, pair_send, pair_recv
        self.send, self.recv, self.half, self.out = send, recv, half, out
        self.sems, self.counts = sems, counts
        self.tiles = own.shape[1]
        self.readers = chips.others

    def by_parity(self, action):
        for odd in range(2):
            pl.when(self.chips.odd == odd)(functools.partial(action, odd))

    def place(self, rank, odd):
        if sum(self.counts) == 3:
            return 3 * (rank // 2) + (rank % 2) * (1 + odd)
        return rank // 2

    def start_pair(self):
        self.pair_send[...] = self.own[1 - self.chips.core].astype(BF)
        remote(self.pair_send, self.pair_recv, self.sems, 0, self.chips.sibling).start()

    def start_scatter(self):
        chips = self.chips
        wait_bytes(self.pair_recv, self.sems.at[1, 0])
        self.send[...] = (self.own[chips.core] + self.pair_recv[...].astype(F32)).astype(BF)

        def go(odd):
            for k in range(self.counts[odd]):
                self.recv[k, chips.rank] = self.send[self.place(chips.rank, odd) + k]
            for turn, rank, target in chips.others:
                theirs = (odd + turn) % 2
                count = self.counts[theirs]
                if count:
                    src = self.send.at[pl.ds(self.place(rank, theirs), count)]
                    dst = self.recv.at[pl.ds(0, count), chips.rank]
                    remote(src, dst, self.sems, 1, target).start()

        self.by_parity(go)

    def start_gather(self):
        chips = self.chips

        def go(odd):
            count = self.counts[odd]
            if not count:
                return
            wait_bytes(self.recv.at[pl.ds(0, count), pl.ds(0, CHIPS - 1)], self.sems.at[1, 1])
            spot = self.place(chips.rank, odd)
            for k in range(count):
                self.half[spot + k] = jnp.sum(self.recv[k].astype(F32), axis=0).astype(BF)
            part = self.half.at[pl.ds(spot, count)]
            for _, _, target in self.readers:
                remote(part, part, self.sems, 3, target).start()

        self.by_parity(go)

    def start_return(self):
        def go(odd):
            wait_bytes(self.pair_send.at[pl.ds(0, self.tiles - self.counts[odd])], self.sems.at[1, 3])

        self.by_parity(go)
        out = self.out.at[self.chips.core]
        remote(self.half, out, self.sems, 4, self.chips.sibling).start()
        pltpu.make_async_copy(self.half, out, self.sems.at[0, 5]).start()

    def sent(self, odd):
        count = self.counts[odd]
        wait_bytes(self.pair_send.at[pl.ds(0, self.tiles - count)], self.sems.at[0, 1])
        if count:
            wait_bytes(self.recv.at[pl.ds(0, count), pl.ds(0, CHIPS - 1)], self.sems.at[0, 3])

    def finish(self):
        wait_bytes(self.pair_send, self.sems.at[0, 0])
        self.by_parity(self.sent)
        wait_bytes(self.pair_send, self.sems.at[0, 4])
        wait_bytes(self.pair_send, self.sems.at[0, 5])
        wait_bytes(self.pair_recv, self.sems.at[1, 4])


class PlaneReducer(Reducer):
    def __init__(self, chips, *refs):
        super().__init__(chips, *refs, (1, 1))
        self.readers = [other for o, other in zip(OFFSETS, chips.others) if o[0] == 0]

    def by_parity(self, action):
        action(0)

    def place(self, rank, odd):
        return rank % 16

    def sent(self, odd):
        wait_bytes(self.recv.at[0, pl.ds(0, CHIPS - 1)], self.sems.at[0, 1])
        wait_bytes(self.recv.at[0, pl.ds(0, len(self.readers))], self.sems.at[0, 3])


class SquareReducer:
    def __init__(self, chips, own, pair, recv, total, out, sems):
        self.chips, self.own, self.pair, self.recv = chips, own, pair, recv
        self.total, self.out, self.sems = total, out, sems

    def start_pair(self):
        remote(self.own, self.pair, self.sems, 0, self.chips.sibling).start()

    def start_scatter(self):
        wait_bytes(self.pair, self.sems.at[1, 0])
        rank = self.chips.rank
        self.recv[rank] = self.own[...] + self.pair[...]
        for _, _, target in self.chips.others:
            remote(self.recv.at[rank], self.recv.at[rank], self.sems, 1, target).start()

    def start_return(self):
        wait_bytes(self.recv.at[pl.ds(0, CHIPS - 1)], self.sems.at[1, 1])
        self.total[...] = jnp.sum(self.recv[...], axis=0)
        pltpu.make_async_copy(self.total, self.out, self.sems.at[0, 2]).start()

    def finish(self):
        wait_bytes(self.own, self.sems.at[0, 0])
        wait_bytes(self.recv.at[pl.ds(0, CHIPS - 1)], self.sems.at[0, 1])
        wait_bytes(self.total, self.sems.at[0, 2])


def tile_spots():
    places = [chip_tiles(r) for r in range(CHIPS)]
    return [s for s, _ in places], [s + 1 for s, n in places if n == 2]


def step_kernel(
    grad_factor,
    samples_in, index_in, targets_in, w_in_in, w_mid_in, w_out_in, v_in_in, v_mid_in, v_out_in,
    branch_out, trunk_out, first_out, square_out,
    samples, index, targets, w_in, w_mid, w_out, v_in, v_mid, v_out,
    feats, t_one, t_two, basis, basis_grad, b_one, b_two, coeff, coeff_t, coeff_grad,
    squares,
    branch_own, branch_pair_send, branch_pair_recv, branch_send, branch_recv, branch_half,
    trunk_own, trunk_pair_send, trunk_pair_recv, trunk_send, trunk_recv, trunk_half,
    first_own, first_pair_send, first_pair_recv, first_send, first_recv, first_half,
    square_own, square_pair, square_recv, square_total,
    local_sems, target_sems, branch_sems, trunk_sems, first_sems, square_sems,
):
    samp, pts = targets.shape
    chunks = target_sems.shape[0]
    chunk = samp // chunks
    chips = Chips()
    branch = Reducer(
        chips, branch_own, branch_pair_send, branch_pair_recv, branch_send, branch_recv,
        branch_half, branch_out, branch_sems, (2, 1),
    )
    trunk = Reducer(
        chips, trunk_own, trunk_pair_send, trunk_pair_recv, trunk_send, trunk_recv,
        trunk_half, trunk_out, trunk_sems, (0, 1),
    )
    first = PlaneReducer(
        chips, first_own, first_pair_send, first_pair_recv, first_send, first_recv,
        first_half, first_out, first_sems,
    )
    square = SquareReducer(
        chips, square_own, square_pair, square_recv, square_total, square_out, square_sems
    )

    loads = []
    for k, (src, dst) in enumerate(
        (
            (index_in, index), (v_in_in, v_in), (v_mid_in, v_mid), (v_out_in, v_out),
            (w_in_in, w_in), (w_mid_in, w_mid), (w_out_in, w_out), (samples_in, samples),
        )
    ):
        copy = pltpu.make_async_copy(src, dst, local_sems.at[k])
        copy.start()
        loads.append(copy)
    target_loads = []
    for k in range(chunks):
        rows = pl.ds(k * chunk, chunk)
        copy = pltpu.make_async_copy(targets_in.at[rows], targets.at[rows], target_sems.at[k])
        copy.start()
        target_loads.append(copy)

    barrier = pltpu.get_barrier_semaphore()

    def greet(target):
        pl.semaphore_signal(barrier, inc=1, device_id=target, device_id_type=MESH)

    greet(chips.sibling)
    for _, _, target in chips.others:
        greet(target)

    for k in range(4):
        loads[k].wait()
    quarter = feats.shape[0] // 4
    v_in_t, v_mid_t, v_out_t = v_in[...].T, v_mid[...].T, v_out[...].T
    wide = 1024
    block = 512
    blocks = pts // block

    def trunk_feats(p):
        cols = pl.ds(p * block, block)
        for axis in range(2):
            turns = (2.0 * index[axis : axis + 1, cols].astype(F32) + 1.0) * (0.25 / GRID_SIDE)
            sines, cosines = waves(turns, quarter)
            base = 2 * axis * quarter
            feats[base : base + quarter, cols] = sines.astype(BF)
            feats[base + quarter : base + 2 * quarter, cols] = cosines.astype(BF)

    def trunk_one(p):
        cols = pl.ds(p * block, block)
        t_one[:, cols] = jnp.tanh(dot(v_in_t, feats[:, cols], 1, 0)).astype(BF)

    def trunk_two(p):
        cols = pl.ds(p * block, block)
        t_two[:, cols] = jnp.tanh(dot(v_mid_t, t_one[:, cols], 1, 0)).astype(BF)

    def trunk_basis(p):
        cols = pl.ds(p * block, block)
        basis[:, cols] = dot(v_out_t, t_two[:, cols], 1, 0).astype(BF)

    quarter_rows = samp // 4

    def branch_one(k):
        rows = pl.ds(k * quarter_rows, quarter_rows)
        b_one[rows, :] = jnp.tanh(dot(samples[rows, :], w_in[...], 1, 0)).astype(BF)

    def branch_two(k):
        rows = pl.ds(k * quarter_rows, quarter_rows)
        b_two[rows, :] = jnp.tanh(dot(b_one[rows, :], w_mid[...], 1, 0)).astype(BF)

    def branch_coeff(k):
        rows = pl.ds(k * quarter_rows, quarter_rows)
        coeff[rows, :] = dot(b_two[rows, :], w_out[...], 1, 0).astype(BF)

    stages = (trunk_feats, trunk_one, trunk_two, trunk_basis)
    branch_stages = (branch_one, branch_two, branch_coeff)
    branch_from = 5
    for step in range(blocks + len(stages) - 1):
        if step == branch_from:
            for k in range(4, 8):
                loads[k].wait()
        for lag, stage in enumerate(stages):
            if 0 <= step - lag < blocks:
                stage(step - lag)
        for lag, stage in enumerate(branch_stages):
            if 0 <= step - branch_from - lag < 4:
                stage(step - branch_from - lag)
    coeff_t[...] = coeff[...].T

    squares[...] = jnp.zeros_like(squares)
    for k in range(chunks):
        rows = pl.ds(k * chunk, chunk)
        target_loads[k].wait()
        scaled = coeff[rows, :] * jnp.asarray(1.0 / 16.0, BF)
        for p in range(0, pts, wide):
            cols = pl.ds(p, wide)
            residual = dot(scaled, basis[:, cols], 1, 0) - targets[rows, cols].astype(F32)
            targets[rows, cols] = (residual * grad_factor).astype(BF)
            squared = residual * residual
            squares[...] += jnp.sum(squared.reshape(chunk // 8, 8, wide), axis=0)
        coeff_grad[rows, :] = dot(targets[rows, :], basis[...], 1, 1).astype(BF)

    grad = coeff_grad[...]
    part_out = dot(b_two[...], grad, 0, 0)
    slope = 1.0 - jnp.square(b_two[...].astype(F32))
    back_two = (dot(grad, w_out[...], 1, 1) * slope).astype(BF)
    part_mid = dot(b_one[...], back_two, 0, 0)
    slope = 1.0 - jnp.square(b_one[...].astype(F32))
    back_one = (dot(back_two, w_mid[...], 1, 1) * slope).astype(BF)
    part_in = dot(samples[...], back_one, 0, 0)
    square_own[...] = jnp.sum(jnp.sum(squares[...].reshape(8, wide // 128, 128), axis=1), axis=0, keepdims=True)

    def pack(own, part, core, spots, row):
        for k, spot in enumerate(spots):
            strip = part[row + 8 * k : row + 8 * k + 8]
            own[core, spot, 0:8] = strip[:, :128]
            own[core, spot, 8:16] = strip[:, 128:]

    singles, doubles = tile_spots()
    for c in range(2):
        pack(branch_own, part_in, c, singles, c * 512)
        pack(branch_own, part_mid, c, doubles[:16], c * 128)
        pack(branch_own, part_out, c, doubles[16:], c * 128)

    pl.semaphore_wait(barrier, CHIPS)
    branch.start_pair()
    square.start_pair()

    for p in range(0, pts, wide):
        cols = pl.ds(p, wide)
        basis_grad[:, cols] = dot(coeff_t[...], targets[:, cols], 1, 0).astype(BF)
        if p == wide:
            branch.start_scatter()
            square.start_scatter()

    def pack_trunk(own, part, spot):
        for c in range(2):
            pack(own, part, c, range(spot, spot + 16), c * 128)

    def back(weight, grad, hidden, result):
        for p in range(0, pts, wide):
            cols = pl.ds(p, wide)
            slope = 1.0 - jnp.square(hidden[:, cols].astype(F32))
            result[:, cols] = (dot(weight[...], grad[:, cols], 1, 0) * slope).astype(BF)

    back_two_t, back_one_t = basis, basis_grad
    pack_trunk(trunk_own, dot(t_two[...], basis_grad[...], 1, 1), 0)
    back(v_out, basis_grad, t_two, back_two_t)
    pack_trunk(trunk_own, dot(t_one[...], back_two_t[...], 1, 1), 16)
    trunk.start_pair()
    back(v_mid, back_two_t, t_one, back_one_t)
    trunk.start_scatter()
    pack_trunk(first_own, dot(feats[...], back_one_t[...], 1, 1), 0)
    first.start_pair()
    first.start_scatter()

    branch.start_gather()
    trunk.start_gather()
    square.start_return()
    first.start_gather()
    branch.start_return()
    trunk.start_return()
    first.start_return()
    trunk.finish()
    branch.finish()
    first.finish()
    square.finish()


def spread_kernel(
    loss_scale, branch_in, trunk_in, first_in, square_in, g_w_in, g_w_mid, g_w_out, g_v_in, g_v_mid, g_v_out, loss_out,
    branch, trunk, first, square, loss, w_in, w_mid, w_out, v_in, v_mid, v_out, in_sems, out_sems,
):
    loads = [
        pltpu.make_async_copy(src, dst, in_sems.at[k])
        for k, (src, dst) in enumerate(
            (
                (branch_in.at[0], branch.at[0]), (branch_in.at[1], branch.at[1]),
                (trunk_in, trunk), (first_in, first), (square_in, square),
            )
        )
    ]
    for load in loads:
        load.start()
    stores = []

    def put(src, c, spots, held, out):
        rows = 8 * len(spots)
        for k, spot in enumerate(spots):
            tile = src[c, spot].astype(F32)
            row = c * rows + 8 * k
            held[row : row + 8, 0:128] = tile[:8]
            held[row : row + 8, 128:256] = tile[8:]
        span = pl.ds(c * rows, rows)
        store = pltpu.make_async_copy(held.at[span], out.at[span], out_sems.at[len(stores)])
        store.start()
        stores.append(store)

    singles, doubles = tile_spots()
    for c in range(2):
        loads[c].wait()
        put(branch, c, singles, w_in, g_w_in)
        put(branch, c, doubles[:16], w_mid, g_w_mid)
        put(branch, c, doubles[16:], w_out, g_w_out)
    loads[2].wait()
    loads[3].wait()
    for c in range(2):
        put(trunk, c, range(16), v_out, g_v_out)
        put(trunk, c, range(16, 32), v_mid, g_v_mid)
        put(first, c, range(16), v_in, g_v_in)
    loads[4].wait()
    loss[...] = jnp.sum(square[...], keepdims=True) * loss_scale
    stores.append(pltpu.make_async_copy(loss, loss_out, out_sems.at[len(stores)]))
    stores[-1].start()
    for store in stores:
        store.wait()


def on_device(samples, point_index, targets, w_in, w_mid, w_out, v_in, v_mid, v_out):
    samp, pts = targets.shape
    total_cells = samp * lax.axis_size("batch") * pts * lax.axis_size("grid")
    sensors, hidden = w_in.shape
    grad_factor = 64.0 / math.sqrt(total_cells) * w_out.shape[1] ** (-0.5)
    chunks = 4
    any_spec = pl.BlockSpec(memory_space=pl.ANY)
    inputs = (samples, point_index, targets, w_in, w_mid, w_out, v_in, v_mid, v_out)
    v = pltpu.VMEM
    scratch = [v(a.shape, a.dtype) for a in inputs]
    scratch += [v((hidden, pts), BF)] * 5
    scratch += [v((samp, hidden), BF)] * 3 + [v((hidden, samp), BF), v((samp, hidden), BF)]
    scratch += [v((8, 1024), F32)]
    for tiles, most in ((BRANCH_TILES, 2), (TRUNK_TILES, 1), (FIRST_TILES, 1)):
        scratch += [
            v((2, tiles, *TILE), F32),
            v((tiles, *TILE), BF),
            v((tiles, *TILE), BF),
            v((tiles, *TILE), BF),
            v((most, CHIPS, *TILE), BF),
            v((tiles, *TILE), BF),
        ]
    scratch += [v((1, 128), F32), v((1, 128), F32), v((CHIPS, 1, 128), F32), v((1, 128), F32)]
    scratch += [
        pltpu.SemaphoreType.DMA((8,)),
        pltpu.SemaphoreType.DMA((chunks,)),
        pltpu.SemaphoreType.DMA((2, 6)),
        pltpu.SemaphoreType.DMA((2, 6)),
        pltpu.SemaphoreType.DMA((2, 6)),
        pltpu.SemaphoreType.DMA((2, 3)),
    ]
    branch, trunk, first, square = pl.pallas_call(
        functools.partial(step_kernel, grad_factor),
        out_shape=(
            jax.ShapeDtypeStruct((2, BRANCH_TILES, *TILE), BF),
            jax.ShapeDtypeStruct((2, TRUNK_TILES, *TILE), BF),
            jax.ShapeDtypeStruct((2, FIRST_TILES, *TILE), BF),
            jax.ShapeDtypeStruct((1, 128), F32),
        ),
        in_specs=[any_spec] * 9,
        out_specs=[any_spec] * 4,
        scratch_shapes=scratch,
        compiler_params=pltpu.CompilerParams(
            collective_id=0, has_side_effects=True, vmem_limit_bytes=58 << 20
        ),
        name="deeponet_step",
    )(*inputs)
    shapes = [(sensors, hidden)] + [(hidden, hidden)] * 5 + [(1, 1)]
    outs = pl.pallas_call(
        functools.partial(spread_kernel, 1.0 / (2.0 * total_cells)),
        out_shape=[jax.ShapeDtypeStruct(s, F32) for s in shapes],
        in_specs=[any_spec] * 4,
        out_specs=[any_spec] * 7,
        scratch_shapes=[v((2, n, *TILE), BF) for n in (BRANCH_TILES, TRUNK_TILES, FIRST_TILES)]
        + [v((1, 128), F32), v((1, 1), F32)]
        + [v(s, F32) for s in shapes[:6]]
        + [pltpu.SemaphoreType.DMA((5,)), pltpu.SemaphoreType.DMA((13,))],
        compiler_params=pltpu.CompilerParams(vmem_limit_bytes=60 << 20),
        name="spread_gradients",
    )(branch, trunk, first, square)
    return (*outs[:6], outs[6].reshape(()))


def solution(mesh):
    placed = (P("batch", None), P(None, "grid"), P("batch", "grid"), P(), P(), P(), P(), P(), P())
    return jax.shard_map(
        on_device,
        mesh=mesh,
        in_specs=placed,
        out_specs=(P(), P(), P(), P(), P(), P(), P()),
        check_vma=False,
    )
```

time: 50.7 us -> 48.5 us (0.957)
  Pallas kernels: 49.8 us -> 47.6 us
    pallas_call x1, Pallas kernels: 46.8 us -> 45 us  [on_device(): pl.pallas_call(functools.partial(step_kernel, grad_factor), out_shape=(ja...]
where the time goes in v3:
time: 48.5 us; the launch traced here: 48.4 us
  Pallas kernels  47.6 us (98%)
  between operations  0.8 us (2%)
    pallas_call x1, Pallas kernels, on_device(): pl.pallas_call(functools.partial(step_kernel, grad_factor), out_shape=(ja...  45 us
    pallas_call x1, Pallas kernels, on_device(): pl.pallas_call(functools.partial(spread_kernel, 1.0 / (2.0 * total_cells)...  2.58 us

profile of v3, /device:TPU:1, one launch (start us, length us, event | category | flops | bytes accessed | tf_op | source)
XLA Modules:
  0.0 48.4 jit_solution(8509174461011159532)
XLA Ops:
  0.6 45.0 %deeponet_step.1 = (bf16[2,96,16,128]{3,2,1,0:T(8,128)(2,1)}, bf16[2,32,16,128]{3,2,1,0:T(8,128)(2,1)}, bf16[2,16,16,128]{3,2,1,0:T(8,128)(2,1)}, f32[1,128]{1,0:T(1,128)}) custom-call(bf16[1024,1024]{1,0:T(8,128)(2,1)} %samples_in.1, s32[2,4096]{1,0:T(2,128)} %index_in.1, bf16[1024,4096]{1,0:T(8,128)(2,1)} %targets_in.1, bf16[1024,256]{1,0:T(8,128)(2,1)} %w_in_in.1, ...), custom_call_target="tpu_custom_call" | custom-call | tf_op jit(solution)/shard_map/deeponet_step/pallas_call | solution.py:514
  45.6 2.6 %spread_gradients.1 = (f32[1024,256]{1,0:T(8,128)}, f32[256,256]{1,0:T(8,128)}, f32[256,256]{1,0:T(8,128)}, f32[256,256]{1,0:T(8,128)}, f32[256,256]{1,0:T(8,128)}, /*index=5*/f32[256,256]{1,0:T(8,128)}, f32[1,1]{1,0:T(1,128)}) custom-call(bf16[2,96,16,128]{3,2,1,0:T(8,128)(2,1)} %get-tuple-element.18.branch_in, ...), custom_call_target="tpu_custom_call" | custom-call | tf_op jit(solution)/shard_map/spread_gradients/pallas_call | solution.py:531

commit v4 on v3

--- a/solution.py
+++ b/solution.py
@@ -77,11 +77,6 @@
 OFFSETS = sorted(
     itertools.product(range(4), repeat=3), key=lambda o: -sum(min(d, 4 - d) for d in o)
 )
-
-
-def chip_tiles(rank):
-    even = (rank // 16 + rank // 4 + rank) % 2 == 0
-    return 3 * (rank // 2) + (rank % 2) * (1 if even else 2), 2 if even else 1
 
 
 class Chips:
@@ -99,12 +94,14 @@
         self.all = [
             (
                 sum(o),
+                (xs[o[0]], ys[o[1]], zs[o[2]]),
                 ranks[0][o[0]] + ranks[1][o[1]] + ranks[2][o[2]],
                 {"batch": batches[0][o[0]] + batches[1][o[2]], "grid": grids[0][o[1]] + grids[1][o[2]]},
             )
             for o in OFFSETS
         ]
         self.others = self.all[:-1]
+        self.place = (self.x, self.y, self.z)
 
 
 class Reducer:
@@ -121,8 +118,6 @@
             pl.when(self.chips.odd == odd)(functools.partial(action, odd))
 
     def place(self, rank, odd):
-        if sum(self.counts) == 3:
-            return 3 * (rank // 2) + (rank % 2) * (1 + odd)
         return rank // 2
 
     def start_pair(self):
@@ -137,7 +132,7 @@
         def go(odd):
             for k in range(self.counts[odd]):
                 self.recv[k, chips.rank] = self.send[self.place(chips.rank, odd) + k]
-            for turn, rank, target in chips.others:
+            for turn, _, rank, target in chips.others:
                 theirs = (odd + turn) % 2
                 count = self.counts[theirs]
                 if count:
@@ -159,7 +154,7 @@
             for k in range(count):
                 self.half[spot + k] = jnp.sum(self.recv[k].astype(F32), axis=0).astype(BF)
             part = self.half.at[pl.ds(spot, count)]
-            for _, _, target in self.readers:
+            for *_, target in self.readers:
                 remote(part, part, self.sems, 3, target).start()
 
         self.by_parity(go)
@@ -187,6 +182,70 @@
         wait_bytes(self.pair_recv, self.sems.at[1, 4])
 
 
+CLASSES = ((0, 2), (1,))
+
+
+def class_spot(place, axis):
+    u, v = (c for k, c in enumerate(place) if k != axis)
+    return 32 * axis + 8 * place[axis] + (u * 4 + v) // 2
+
+
+class BranchReducer(Reducer):
+    def start_scatter(self):
+        chips = self.chips
+        wait_bytes(self.pair_recv, self.sems.at[1, 0])
+        self.send[...] = (self.own[chips.core] + self.pair_recv[...].astype(F32)).astype(BF)
+
+        def go(odd):
+            for k, axis in enumerate(CLASSES[odd]):
+                self.recv[k, chips.rank] = self.send[class_spot(chips.place, axis)]
+            for turn, place, _, target in chips.others:
+                for k, axis in enumerate(CLASSES[(odd + turn) % 2]):
+                    src, dst = self.send.at[class_spot(place, axis)], self.recv.at[k, chips.rank]
+                    remote(src, dst, self.sems, 1, target).start()
+
+        self.by_parity(go)
+
+    def start_gather(self):
+        chips = self.chips
+
+        def go(odd):
+            count = self.counts[odd]
+            wait_bytes(self.recv.at[pl.ds(0, count), pl.ds(0, CHIPS - 1)], self.sems.at[1, 1])
+            for k, axis in enumerate(CLASSES[odd]):
+                spot = class_spot(chips.place, axis)
+                self.half[spot] = jnp.sum(self.recv[k].astype(F32), axis=0).astype(BF)
+                part = self.half.at[spot]
+                for o, (*_, target) in zip(OFFSETS, chips.others):
+                    if o[axis] == 0:
+                        remote(part, part, self.sems, 3, target).start()
+
+        self.by_parity(go)
+
+    def start_line(self):
+        def go(odd):
+            wait_bytes(self.pair_send.at[pl.ds(0, 24 - self.counts[odd])], self.sems.at[1, 3])
+
+        self.by_parity(go)
+        for o, (*_, target) in zip(OFFSETS, self.chips.others):
+            if o.count(0) == 2:
+                axis = next(k for k in range(3) if o[k])
+                part = self.half.at[pl.ds(32 * axis + 8 * self.chips.place[axis], 8)]
+                remote(part, part, self.sems, 6, target).start()
+
+    def start_return(self):
+        wait_bytes(self.pair_send.at[pl.ds(0, 72)], self.sems.at[1, 6])
+        out = self.out.at[self.chips.core]
+        remote(self.half, out, self.sems, 4, self.chips.sibling).start()
+        pltpu.make_async_copy(self.half, out, self.sems.at[0, 5]).start()
+
+    def sent(self, odd):
+        count = self.counts[odd]
+        wait_bytes(self.pair_send.at[pl.ds(0, self.tiles - count)], self.sems.at[0, 1])
+        wait_bytes(self.recv.at[pl.ds(0, count), pl.ds(0, 15)], self.sems.at[0, 3])
+        wait_bytes(self.pair_send.at[pl.ds(0, 72)], self.sems.at[0, 6])
+
+
 class PlaneReducer(Reducer):
     def __init__(self, chips, *refs):
         super().__init__(chips, *refs, (1, 1))
@@ -215,7 +274,7 @@
         wait_bytes(self.pair, self.sems.at[1, 0])
         rank = self.chips.rank
         self.recv[rank] = self.own[...] + self.pair[...]
-        for _, _, target in self.chips.others:
+        for *_, target in self.chips.others:
             remote(self.recv.at[rank], self.recv.at[rank], self.sems, 1, target).start()
 
     def start_return(self):
@@ -230,8 +289,12 @@
 
 
 def tile_spots():
-    places = [chip_tiles(r) for r in range(CHIPS)]
-    return [s for s, _ in places], [s + 1 for s, n in places if n == 2]
+    singles, doubles = [], []
+    for place in itertools.product(range(4), repeat=3):
+        axes = CLASSES[sum(place) % 2]
+        singles.append(class_spot(place, axes[0]))
+        doubles += [class_spot(place, axis) for axis in axes[1:]]
+    return singles, doubles
 
 
 def step_kernel(
@@ -251,7 +314,7 @@
     chunks = target_sems.shape[0]
     chunk = samp // chunks
     chips = Chips()
-    branch = Reducer(
+    branch = BranchReducer(
         chips, branch_own, branch_pair_send, branch_pair_recv, branch_send, branch_recv,
         branch_half, branch_out, branch_sems, (2, 1),
     )
@@ -290,7 +353,7 @@
         pl.semaphore_signal(barrier, inc=1, device_id=target, device_id_type=MESH)
 
     greet(chips.sibling)
-    for _, _, target in chips.others:
+    for *_, target in chips.others:
         greet(target)
 
     for k in range(4):
@@ -422,9 +485,10 @@
     trunk.start_gather()
     square.start_return()
     first.start_gather()
-    branch.start_return()
+    branch.start_line()
     trunk.start_return()
     first.start_return()
+    branch.start_return()
     trunk.finish()
     branch.finish()
     first.finish()
@@ -485,7 +549,7 @@
     total_cells = samp * lax.axis_size("batch") * pts * lax.axis_size("grid")
     sensors, hidden = w_in.shape
     grad_factor = 64.0 / math.sqrt(total_cells) * w_out.shape[1] ** (-0.5)
-    chunks = 4
+    chunks = 2
     any_spec = pl.BlockSpec(memory_space=pl.ANY)
     inputs = (samples, point_index, targets, w_in, w_mid, w_out, v_in, v_mid, v_out)
     v = pltpu.VMEM
@@ -506,7 +570,7 @@
     scratch += [
         pltpu.SemaphoreType.DMA((8,)),
         pltpu.SemaphoreType.DMA((chunks,)),
-        pltpu.SemaphoreType.DMA((2, 6)),
+        pltpu.SemaphoreType.DMA((2, 7)),
         pltpu.SemaphoreType.DMA((2, 6)),
         pltpu.SemaphoreType.DMA((2, 6)),
         pltpu.SemaphoreType.DMA((2, 3)),

time: 48.5 us -> 48.1 us (level)
  Pallas kernels: 47.6 us -> 47.1 us
where the time goes in v4:
time: 48.1 us; the launch traced here: 47.9 us
  Pallas kernels  47.1 us (98%)
  between operations  0.8 us (2%)
    pallas_call x1, Pallas kernels, on_device(): pl.pallas_call(functools.partial(step_kernel, grad_factor), out_shape=(ja...  44.6 us
    pallas_call x1, Pallas kernels, on_device(): pl.pallas_call(functools.partial(spread_kernel, 1.0 / (2.0 * total_cells)...  2.58 us

profile of v4, /device:TPU:1, one launch (start us, length us, event | category | flops | bytes accessed | tf_op | source)
XLA Modules:
  0.0 47.9 jit_solution(9186946526543240905)
XLA Ops:
  0.6 44.6 %deeponet_step.1 = (bf16[2,96,16,128]{3,2,1,0:T(8,128)(2,1)}, bf16[2,32,16,128]{3,2,1,0:T(8,128)(2,1)}, bf16[2,16,16,128]{3,2,1,0:T(8,128)(2,1)}, f32[1,128]{1,0:T(1,128)}) custom-call(bf16[1024,1024]{1,0:T(8,128)(2,1)} %samples_in.1, s32[2,4096]{1,0:T(2,128)} %index_in.1, bf16[1024,4096]{1,0:T(8,128)(2,1)} %targets_in.1, bf16[1024,256]{1,0:T(8,128)(2,1)} %w_in_in.1, ...), custom_call_target="tpu_custom_call" | custom-call | tf_op jit(solution)/shard_map/deeponet_step/pallas_call | solution.py:578
  45.2 2.6 %spread_gradients.1 = (f32[1024,256]{1,0:T(8,128)}, f32[256,256]{1,0:T(8,128)}, f32[256,256]{1,0:T(8,128)}, f32[256,256]{1,0:T(8,128)}, f32[256,256]{1,0:T(8,128)}, /*index=5*/f32[256,256]{1,0:T(8,128)}, f32[1,1]{1,0:T(1,128)}) custom-call(bf16[2,96,16,128]{3,2,1,0:T(8,128)(2,1)} %get-tuple-element.18.branch_in, ...), custom_call_target="tpu_custom_call" | custom-call | tf_op jit(solution)/shard_map/spread_gradients/pallas_call | solution.py:595

commit v5 on v4

--- a/solution.py
+++ b/solution.py
@@ -263,8 +263,8 @@
 
 
 class SquareReducer:
-    def __init__(self, chips, own, pair, recv, total, out, sems):
-        self.chips, self.own, self.pair, self.recv = chips, own, pair, recv
+    def __init__(self, chips, own, pair, recv, line, total, out, sems):
+        self.chips, self.own, self.pair, self.recv, self.line = chips, own, pair, recv, line
         self.total, self.out, self.sems = total, out, sems
 
     def start_pair(self):
@@ -272,20 +272,30 @@
 
     def start_scatter(self):
         wait_bytes(self.pair, self.sems.at[1, 0])
-        rank = self.chips.rank
-        self.recv[rank] = self.own[...] + self.pair[...]
-        for *_, target in self.chips.others:
-            remote(self.recv.at[rank], self.recv.at[rank], self.sems, 1, target).start()
+        slot = self.recv.at[self.chips.rank % 16]
+        slot[...] = self.own[...] + self.pair[...]
+        for o, (*_, target) in zip(OFFSETS, self.chips.others):
+            if o[0] == 0:
+                remote(slot, slot, self.sems, 1, target).start()
+
+    def start_line(self):
+        wait_bytes(self.recv.at[pl.ds(0, 15)], self.sems.at[1, 1])
+        slot = self.line.at[self.chips.x]
+        slot[...] = jnp.sum(self.recv[...], axis=0)
+        for o, (*_, target) in zip(OFFSETS, self.chips.others):
+            if o[1:] == (0, 0):
+                remote(slot, slot, self.sems, 2, target).start()
 
     def start_return(self):
-        wait_bytes(self.recv.at[pl.ds(0, CHIPS - 1)], self.sems.at[1, 1])
-        self.total[...] = jnp.sum(self.recv[...], axis=0)
-        pltpu.make_async_copy(self.total, self.out, self.sems.at[0, 2]).start()
+        wait_bytes(self.line.at[pl.ds(0, 3)], self.sems.at[1, 2])
+        self.total[...] = (self.line[0] + self.line[1]) + (self.line[2] + self.line[3])
+        pltpu.make_async_copy(self.total, self.out, self.sems.at[0, 3]).start()
 
     def finish(self):
         wait_bytes(self.own, self.sems.at[0, 0])
-        wait_bytes(self.recv.at[pl.ds(0, CHIPS - 1)], self.sems.at[0, 1])
-        wait_bytes(self.total, self.sems.at[0, 2])
+        wait_bytes(self.recv.at[pl.ds(0, 15)], self.sems.at[0, 1])
+        wait_bytes(self.line.at[pl.ds(0, 3)], self.sems.at[0, 2])
+        wait_bytes(self.total, self.sems.at[0, 3])
 
 
 def tile_spots():
@@ -307,7 +317,7 @@
     branch_own, branch_pair_send, branch_pair_recv, branch_send, branch_recv, branch_half,
     trunk_own, trunk_pair_send, trunk_pair_recv, trunk_send, trunk_recv, trunk_half,
     first_own, first_pair_send, first_pair_recv, first_send, first_recv, first_half,
-    square_own, square_pair, square_recv, square_total,
+    square_own, square_pair, square_recv, square_line, square_total,
     local_sems, target_sems, branch_sems, trunk_sems, first_sems, square_sems,
 ):
     samp, pts = targets.shape
@@ -327,7 +337,8 @@
         first_half, first_out, first_sems,
     )
     square = SquareReducer(
-        chips, square_own, square_pair, square_recv, square_total, square_out, square_sems
+        chips, square_own, square_pair, square_recv, square_line, square_total, square_out,
+        square_sems,
     )
 
     loads = []
@@ -481,6 +492,7 @@
     first.start_pair()
     first.start_scatter()
 
+    square.start_line()
     branch.start_gather()
     trunk.start_gather()
     square.start_return()
@@ -566,14 +578,15 @@
             v((most, CHIPS, *TILE), BF),
             v((tiles, *TILE), BF),
         ]
-    scratch += [v((1, 128), F32), v((1, 128), F32), v((CHIPS, 1, 128), F32), v((1, 128), F32)]
+    scratch += [v((1, 128), F32), v((1, 128), F32), v((16, 1, 128), F32), v((4, 1, 128), F32)]
+    scratch += [v((1, 128), F32)]
     scratch += [
         pltpu.SemaphoreType.DMA((8,)),
         pltpu.SemaphoreType.DMA((chunks,)),
         pltpu.SemaphoreType.DMA((2, 7)),
         pltpu.SemaphoreType.DMA((2, 6)),
         pltpu.SemaphoreType.DMA((2, 6)),
-        pltpu.SemaphoreType.DMA((2, 3)),
+        pltpu.SemaphoreType.DMA((2, 4)),
     ]
     branch, trunk, first, square = pl.pallas_call(
         functools.partial(step_kernel, grad_factor),

time: 48.1 us -> 47.9 us (level)
  no operation moved by 1% of the time
where the time goes in v5:
time: 47.9 us; the launch traced here: 47.7 us
  Pallas kernels  46.9 us (98%)
  between operations  0.8 us (2%)
    pallas_call x1, Pallas kernels, on_device(): pl.pallas_call(functools.partial(step_kernel, grad_factor), out_shape=(ja...  44.4 us
    pallas_call x1, Pallas kernels, on_device(): pl.pallas_call(functools.partial(spread_kernel, 1.0 / (2.0 * total_cells)...  2.58 us

profile of v5, /device:TPU:1, one launch (start us, length us, event | category | flops | bytes accessed | tf_op | source)
XLA Modules:
  0.0 47.7 jit_solution(14126077527211378579)
XLA Ops:
  0.6 44.4 %deeponet_step.1 = (bf16[2,96,16,128]{3,2,1,0:T(8,128)(2,1)}, bf16[2,32,16,128]{3,2,1,0:T(8,128)(2,1)}, bf16[2,16,16,128]{3,2,1,0:T(8,128)(2,1)}, f32[1,128]{1,0:T(1,128)}) custom-call(bf16[1024,1024]{1,0:T(8,128)(2,1)} %samples_in.1, s32[2,4096]{1,0:T(2,128)} %index_in.1, bf16[1024,4096]{1,0:T(8,128)(2,1)} %targets_in.1, bf16[1024,256]{1,0:T(8,128)(2,1)} %w_in_in.1, ...), custom_call_target="tpu_custom_call" | custom-call | tf_op jit(solution)/shard_map/deeponet_step/pallas_call | solution.py:591
  45.0 2.6 %spread_gradients.1 = (f32[1024,256]{1,0:T(8,128)}, f32[256,256]{1,0:T(8,128)}, f32[256,256]{1,0:T(8,128)}, f32[256,256]{1,0:T(8,128)}, f32[256,256]{1,0:T(8,128)}, /*index=5*/f32[256,256]{1,0:T(8,128)}, f32[1,1]{1,0:T(1,128)}) custom-call(bf16[2,96,16,128]{3,2,1,0:T(8,128)(2,1)} %get-tuple-element.18.branch_in, ...), custom_call_target="tpu_custom_call" | custom-call | tf_op jit(solution)/shard_map/spread_gradients/pallas_call | solution.py:608
